TPU v7x, 32 devices: a whole 2x2x4 slice. The times are simulated.
32 devices in a mesh: row: 4 (over x, core), col: 8 (over z, y).
Axes of the slice: x: 2, y: 2, z: 4, core: 2. Of those that a mesh axis runs over, the one named last changes fastest.
Arguments:
- a_blocks: bfloat16 [4, 8, 24, 4096], P('row', 'col'), may hold values from -1.1953125 to 1.1953125
- b_blocks: bfloat16 [4, 8, 24, 4096], P('row', 'col'), may hold values from -1.1953125 to 1.1953125
- products: int32 [4, 8, 2, 3, 384], P('row', 'col'), may hold values from 0 to 32, as said below
Outputs:
- product: float32 [4, 8, 32, 4096], P('row', 'col')
- norm_sq: float32 [], replicated
Inputs may be any that keep to these rules, and one draw needn't show every extreme that they name: `products`: left and right slots lie below 24; a product slot of 32 marks an unused entry; in every draw some grid position uses all 384 entries in some step, and every position uses at least a third of them.
All inputs are finite; a program needn't handle non-finite values.
Results may differ from a plain program's by a relative error of at most 0.0003.
Values may be sent and summed in bfloat16 or wider, within the bound.
No kernel may reach another device: no remote copies, remote signals or barrier semaphores. Data moves between devices by JAX's collectives and lax.ppermute only.
A program may use at most 64 MiB of HBM per device.

v0:
```python
import jax
import jax.numpy as jnp
from jax import lax
from jax.sharding import PartitionSpec as P

BS = 64
NNZ = 24
GROUPS = 4
NC = 32


def passed_along(block, axis, distance):
    devices = range(lax.axis_size(axis))
    route = [((i - distance) % len(devices), i) for i in devices]
    return lax.ppermute(block, axis, route)


def accumulate(left_tile, right_tile, slots):
    left_all = left_tile.reshape(-1, BS, BS)
    right_all = right_tile.reshape(-1, BS, BS)
    grouped = jnp.transpose(slots.reshape(3, GROUPS, -1), (1, 0, 2))

    def add_group(total, group):
        left = jnp.take(left_all, group[0], axis=0)
        right = jnp.take(right_all, group[1], axis=0)
        blocks = jnp.einsum(
            "pik,pkj->pij", left, right, preferred_element_type=jnp.float32
        ).reshape(-1, BS * BS)
        return (total + jax.ops.segment_sum(blocks, group[2], num_segments=NC), None)

    total, _ = lax.scan(add_group, jnp.zeros((NC, BS * BS), jnp.float32), grouped)
    return total


def move_panels(a_blocks, b_blocks):
    a_moved = passed_along(a_blocks, "col", -1)
    b_moved = passed_along(b_blocks, "row", -1)
    return (a_moved, b_moved)


def global_squares(a_here):
    flat = a_here.reshape(-1)
    local_sum = jnp.dot(flat, flat, preferred_element_type=jnp.float32)
    scale = jnp.float32(1.0 / (lax.axis_size("row") * lax.axis_size("col") * NNZ * BS))
    return lax.psum(local_sum, ("row", "col")) * scale


def per_device(a_blocks, b_blocks, products):
    a_here = a_blocks[0, 0]
    b_here = b_blocks[0, 0]
    slots = products[0, 0]
    norm_sq = global_squares(a_here)
    first = accumulate(a_here, b_here, slots[0])
    a_moved, b_moved = move_panels(a_blocks, b_blocks)
    second = accumulate(a_moved[0, 0], b_moved[0, 0], slots[1])
    product = (first + second).reshape(1, 1, NC, BS * BS)
    return (product, norm_sq)


def solution(mesh):
    return jax.shard_map(
        per_device,
        mesh=mesh,
        in_specs=(
            P("row", "col", None, None),
            P("row", "col", None, None),
            P("row", "col", None, None, None),
        ),
        out_specs=(P("row", "col", None, None), P()),
        check_vma=False,
    )
```

profile of v0, /device:TPU:0, one launch (start us, length us, event | category | flops | bytes accessed | tf_op | source)
XLA Modules:
  0.0 175.6 jit_solution(7042752467235832456)
XLA Ops:
  0.6 6.1 %collective-permute-start = (bf16[1,1,24,4096]{3,2,1,0:T(8,128)(2,1)}, bf16[1,1,24,4096]{3,2,1,0:T(8,128)(2,1)}, u32[]{:S(2)}, u32[]{:S(2)}) collective-permute-start(bf16[1,1,24,4096]{3,2,1,0:T(8,128)(2,1)} %param.9), channel_id=1, source_target_pairs={{1,0},{2,1},{3,2},{4,3},{5,4},{6,5},{7,6},{0,7},{9,8},{10,9},{11,1... | collective-permute-start | bytes 589832 | tf_op jit(solution)/shard_map/ppermute | solution.py:15
  8.7 1.3 reshape_squeeze.21
  10.0 1.6 fusion.20
  12.6 60.2 %while.20 = (s32[]{:T(128)}, f32[32,4096]{1,0:T(8,128)S(1)}, s32[4,3,96]{2,0,1:T(4,128)S(1)}, bf16[24,64,64]{2,1,0:T(8,128)(2,1)S(1)}, bf16[24,64,64]{2,1,0:T(8,...) while((s32[]{:T(128)}, f32[32,4096]{1,0:T(8,128)S(1)}, s32[4,3,96]{2,0,1:T(4,128)S(1)}, ...), condition=%wide.region_2.0_spmd, body=%wide.region_0.3_spmd.sunk | while | flops 51514500 | bytes 17314436 | solution.py:31
  13.5 1.9 %gather_fusion.1 = bf16[96,64,64]{2,1,0:T(8,128)(2,1)} fusion(bf16[24,64,64]{2,1,0:T(8,128)(2,1)S(1)} %get-tuple-element.224, s32[1024]{0:T(1024)S(1)} %get-tuple-element.189), kind=kCustom, calls=%fused_computation.clone.clone.1 | custom fusion | bytes 1573248 | tf_op jit(solution)/shard_map/while/body/eval_jaxpr/jit(_take)/gather | solution.py:24
  15.4 3.7 %fusion.32 = f32[96,64,64]{2,1,0:T(8,128)} fusion(bf16[96,64,64]{2,1,0:T(8,128)(2,1)S(1)} %gather_fusion, bf16[96,64,64]{2,1,0:T(8,128)(2,1)} %gather_fusion.1, pred[96]{0:T(512)(128)(4,1)S(1)} %get-tuple-element.190, pred[96]{0:T(512)(128)(4,1)S(1)} %get-tuple-element.191), kind=kOutput, calls=%fused_computation.6.clone.1 | convolution fusion | flops 51118080 | bytes 3145920 | tf_op jit(solution)/shard_map/while/body/eval_jaxpr/pik,pkj->pij/dot_general | solution.py:26
  19.1 3.1 %copy.31 = f32[96,64,64]{0,2,1:T(8,128)S(1)} copy(f32[96,64,64]{2,1,0:T(8,128)} %fusion.32) | data formatting | bytes 3145728 | tf_op jit(solution)/shard_map/while/body/eval_jaxpr/pik,pkj->pij/dot_general | solution.py:26
  22.2 1.7 copy.32
  23.9 3.7 %scatter_fusion = f32[32,4096]{1,0:T(8,128)S(1)} fusion(f32[32,4096]{1,0:T(8,128)S(1)} %get-tuple-element.213, s32[96]{0:T(128)S(1)} %fusion.31, f32[96,4096]{1,0:T(8,128)} %copy.32), kind=kCustom, calls=%fused_computation.4.clone.1 | custom fusion | flops 393216 | bytes 4718976 | tf_op jit(solution)/shard_map/while/body/eval_jaxpr/scatter-add | solution.py:29
  28.5 1.9 %gather_fusion.1 = bf16[96,64,64]{2,1,0:T(8,128)(2,1)} fusion(bf16[24,64,64]{2,1,0:T(8,128)(2,1)S(1)} %get-tuple-element.224, s32[1024]{0:T(1024)S(1)} %get-tuple-element.189), kind=kCustom, calls=%fused_computation.clone.clone.1 | custom fusion | bytes 1573248 | tf_op jit(solution)/shard_map/while/body/eval_jaxpr/jit(_take)/gather | solution.py:24
  30.5 3.7 %fusion.32 = f32[96,64,64]{2,1,0:T(8,128)} fusion(bf16[96,64,64]{2,1,0:T(8,128)(2,1)S(1)} %gather_fusion, bf16[96,64,64]{2,1,0:T(8,128)(2,1)} %gather_fusion.1, pred[96]{0:T(512)(128)(4,1)S(1)} %get-tuple-element.190, pred[96]{0:T(512)(128)(4,1)S(1)} %get-tuple-element.191), kind=kOutput, calls=%fused_computation.6.clone.1 | convolution fusion | flops 51118080 | bytes 3145920 | tf_op jit(solution)/shard_map/while/body/eval_jaxpr/pik,pkj->pij/dot_general | solution.py:26
  34.2 3.1 %copy.31 = f32[96,64,64]{0,2,1:T(8,128)S(1)} copy(f32[96,64,64]{2,1,0:T(8,128)} %fusion.32) | data formatting | bytes 3145728 | tf_op jit(solution)/shard_map/while/body/eval_jaxpr/pik,pkj->pij/dot_general | solution.py:26
  37.3 1.7 copy.32
  39.0 3.7 %scatter_fusion = f32[32,4096]{1,0:T(8,128)S(1)} fusion(f32[32,4096]{1,0:T(8,128)S(1)} %get-tuple-element.213, s32[96]{0:T(128)S(1)} %fusion.31, f32[96,4096]{1,0:T(8,128)} %copy.32), kind=kCustom, calls=%fused_computation.4.clone.1 | custom fusion | flops 393216 | bytes 4718976 | tf_op jit(solution)/shard_map/while/body/eval_jaxpr/scatter-add | solution.py:29
  43.6 1.9 %gather_fusion.1 = bf16[96,64,64]{2,1,0:T(8,128)(2,1)} fusion(bf16[24,64,64]{2,1,0:T(8,128)(2,1)S(1)} %get-tuple-element.224, s32[1024]{0:T(1024)S(1)} %get-tuple-element.189), kind=kCustom, calls=%fused_computation.clone.clone.1 | custom fusion | bytes 1573248 | tf_op jit(solution)/shard_map/while/body/eval_jaxpr/jit(_take)/gather | solution.py:24
  45.5 3.7 %fusion.32 = f32[96,64,64]{2,1,0:T(8,128)} fusion(bf16[96,64,64]{2,1,0:T(8,128)(2,1)S(1)} %gather_fusion, bf16[96,64,64]{2,1,0:T(8,128)(2,1)} %gather_fusion.1, pred[96]{0:T(512)(128)(4,1)S(1)} %get-tuple-element.190, pred[96]{0:T(512)(128)(4,1)S(1)} %get-tuple-element.191), kind=kOutput, calls=%fused_computation.6.clone.1 | convolution fusion | flops 51118080 | bytes 3145920 | tf_op jit(solution)/shard_map/while/body/eval_jaxpr/pik,pkj->pij/dot_general | solution.py:26
  49.2 3.1 %copy.31 = f32[96,64,64]{0,2,1:T(8,128)S(1)} copy(f32[96,64,64]{2,1,0:T(8,128)} %fusion.32) | data formatting | bytes 3145728 | tf_op jit(solution)/shard_map/while/body/eval_jaxpr/pik,pkj->pij/dot_general | solution.py:26
  52.3 1.7 copy.32
  54.0 3.7 %scatter_fusion = f32[32,4096]{1,0:T(8,128)S(1)} fusion(f32[32,4096]{1,0:T(8,128)S(1)} %get-tuple-element.213, s32[96]{0:T(128)S(1)} %fusion.31, f32[96,4096]{1,0:T(8,128)} %copy.32), kind=kCustom, calls=%fused_computation.4.clone.1 | custom fusion | flops 393216 | bytes 4718976 | tf_op jit(solution)/shard_map/while/body/eval_jaxpr/scatter-add | solution.py:29
  58.6 1.9 %gather_fusion.1 = bf16[96,64,64]{2,1,0:T(8,128)(2,1)} fusion(bf16[24,64,64]{2,1,0:T(8,128)(2,1)S(1)} %get-tuple-element.224, s32[1024]{0:T(1024)S(1)} %get-tuple-element.189), kind=kCustom, calls=%fused_computation.clone.clone.1 | custom fusion | bytes 1573248 | tf_op jit(solution)/shard_map/while/body/eval_jaxpr/jit(_take)/gather | solution.py:24
  60.5 3.7 %fusion.32 = f32[96,64,64]{2,1,0:T(8,128)} fusion(bf16[96,64,64]{2,1,0:T(8,128)(2,1)S(1)} %gather_fusion, bf16[96,64,64]{2,1,0:T(8,128)(2,1)} %gather_fusion.1, pred[96]{0:T(512)(128)(4,1)S(1)} %get-tuple-element.190, pred[96]{0:T(512)(128)(4,1)S(1)} %get-tuple-element.191), kind=kOutput, calls=%fused_computation.6.clone.1 | convolution fusion | flops 51118080 | bytes 3145920 | tf_op jit(solution)/shard_map/while/body/eval_jaxpr/pik,pkj->pij/dot_general | solution.py:26
  64.3 3.1 %copy.31 = f32[96,64,64]{0,2,1:T(8,128)S(1)} copy(f32[96,64,64]{2,1,0:T(8,128)} %fusion.32) | data formatting | bytes 3145728 | tf_op jit(solution)/shard_map/while/body/eval_jaxpr/pik,pkj->pij/dot_general | solution.py:26
  67.3 1.7 copy.32
  69.1 3.7 %scatter_fusion = f32[32,4096]{1,0:T(8,128)S(1)} fusion(f32[32,4096]{1,0:T(8,128)S(1)} %get-tuple-element.213, s32[96]{0:T(128)S(1)} %fusion.31, f32[96,4096]{1,0:T(8,128)} %copy.32), kind=kCustom, calls=%fused_computation.4.clone.1 | custom fusion | flops 393216 | bytes 4718976 | tf_op jit(solution)/shard_map/while/body/eval_jaxpr/scatter-add | solution.py:29
  72.7 37.1 %psum.7 = f32[]{:T(128)} all-reduce(f32[]{:T(128)} %fusion.20), channel_id=1, replica_groups=mesh['row'=4,'col'=8] {'row','col'}, use_global_device_ids=true, to_apply=%region_6.8 | all-reduce | flops 1 | bytes 8 | tf_op jit(solution)/shard_map/psum | solution.py:45
  110.6 1.3 reshape_squeeze.23
  112.0 1.3 reshape_squeeze.24
  113.3 60.3 %while.21 = (s32[]{:T(128)}, f32[32,4096]{1,0:T(8,128)S(1)}, s32[4,3,96]{2,0,1:T(4,128)S(1)}, bf16[24,64,64]{2,1,0:T(8,128)(2,1)S(1)}, bf16[24,64,64]{2,1,0:T(8,...) while((s32[]{:T(128)}, f32[32,4096]{1,0:T(8,128)S(1)}, s32[4,3,96]{2,0,1:T(4,128)S(1)}, ...), condition=%wide.region_5.7_spmd, body=%wide.region_3.0_spmd.sunk | while | flops 51514500 | bytes 18887356 | solution.py:31
  114.3 1.9 %gather_fusion.3 = bf16[96,64,64]{2,1,0:T(8,128)(2,1)} fusion(bf16[24,64,64]{2,1,0:T(8,128)(2,1)S(1)} %get-tuple-element.251, s32[1024]{0:T(1024)S(1)} %get-tuple-element.200), kind=kCustom, calls=%fused_computation.2.clone.clone.1 | custom fusion | bytes 1573248 | tf_op jit(solution)/shard_map/while/body/eval_jaxpr/jit(_take)/gather | solution.py:24
  116.2 3.7 %fusion.36 = f32[96,64,64]{2,1,0:T(8,128)} fusion(bf16[96,64,64]{2,1,0:T(8,128)(2,1)S(1)} %gather_fusion.2, bf16[96,64,64]{2,1,0:T(8,128)(2,1)} %gather_fusion.3, pred[96]{0:T(512)(128)(4,1)S(1)} %get-tuple-element.201, pred[96]{0:T(512)(128)(4,1)S(1)} %get-tuple-element.202), kind=kOutput, calls=%fused_computation.25.clone.1 | convolution fusion | flops 51118080 | bytes 3145920 | tf_op jit(solution)/shard_map/while/body/eval_jaxpr/pik,pkj->pij/dot_general | solution.py:26
  119.9 3.1 %copy.33 = f32[96,64,64]{0,2,1:T(8,128)S(1)} copy(f32[96,64,64]{2,1,0:T(8,128)} %fusion.36) | data formatting | bytes 3145728 | tf_op jit(solution)/shard_map/while/body/eval_jaxpr/pik,pkj->pij/dot_general | solution.py:26
  123.0 1.7 copy.34
  124.7 3.7 %scatter_fusion.1 = f32[32,4096]{1,0:T(8,128)S(1)} fusion(f32[32,4096]{1,0:T(8,128)S(1)} %get-tuple-element.240, s32[96]{0:T(128)S(1)} %fusion.35, f32[96,4096]{1,0:T(8,128)} %copy.34), kind=kCustom, calls=%fused_computation.5.clone.1 | custom fusion | flops 393216 | bytes 4718976 | tf_op jit(solution)/shard_map/while/body/eval_jaxpr/scatter-add | solution.py:29
  129.4 1.9 %gather_fusion.3 = bf16[96,64,64]{2,1,0:T(8,128)(2,1)} fusion(bf16[24,64,64]{2,1,0:T(8,128)(2,1)S(1)} %get-tuple-element.251, s32[1024]{0:T(1024)S(1)} %get-tuple-element.200), kind=kCustom, calls=%fused_computation.2.clone.clone.1 | custom fusion | bytes 1573248 | tf_op jit(solution)/shard_map/while/body/eval_jaxpr/jit(_take)/gather | solution.py:24
  131.3 3.7 %fusion.36 = f32[96,64,64]{2,1,0:T(8,128)} fusion(bf16[96,64,64]{2,1,0:T(8,128)(2,1)S(1)} %gather_fusion.2, bf16[96,64,64]{2,1,0:T(8,128)(2,1)} %gather_fusion.3, pred[96]{0:T(512)(128)(4,1)S(1)} %get-tuple-element.201, pred[96]{0:T(512)(128)(4,1)S(1)} %get-tuple-element.202), kind=kOutput, calls=%fused_computation.25.clone.1 | convolution fusion | flops 51118080 | bytes 3145920 | tf_op jit(solution)/shard_map/while/body/eval_jaxpr/pik,pkj->pij/dot_general | solution.py:26
  135.0 3.1 %copy.33 = f32[96,64,64]{0,2,1:T(8,128)S(1)} copy(f32[96,64,64]{2,1,0:T(8,128)} %fusion.36) | data formatting | bytes 3145728 | tf_op jit(solution)/shard_map/while/body/eval_jaxpr/pik,pkj->pij/dot_general | solution.py:26
  138.1 1.7 copy.34
  139.8 3.7 %scatter_fusion.1 = f32[32,4096]{1,0:T(8,128)S(1)} fusion(f32[32,4096]{1,0:T(8,128)S(1)} %get-tuple-element.240, s32[96]{0:T(128)S(1)} %fusion.35, f32[96,4096]{1,0:T(8,128)} %copy.34), kind=kCustom, calls=%fused_computation.5.clone.1 | custom fusion | flops 393216 | bytes 4718976 | tf_op jit(solution)/shard_map/while/body/eval_jaxpr/scatter-add | solution.py:29
  144.4 1.9 %gather_fusion.3 = bf16[96,64,64]{2,1,0:T(8,128)(2,1)} fusion(bf16[24,64,64]{2,1,0:T(8,128)(2,1)S(1)} %get-tuple-element.251, s32[1024]{0:T(1024)S(1)} %get-tuple-element.200), kind=kCustom, calls=%fused_computation.2.clone.clone.1 | custom fusion | bytes 1573248 | tf_op jit(solution)/shard_map/while/body/eval_jaxpr/jit(_take)/gather | solution.py:24
  146.4 3.7 %fusion.36 = f32[96,64,64]{2,1,0:T(8,128)} fusion(bf16[96,64,64]{2,1,0:T(8,128)(2,1)S(1)} %gather_fusion.2, bf16[96,64,64]{2,1,0:T(8,128)(2,1)} %gather_fusion.3, pred[96]{0:T(512)(128)(4,1)S(1)} %get-tuple-element.201, pred[96]{0:T(512)(128)(4,1)S(1)} %get-tuple-element.202), kind=kOutput, calls=%fused_computation.25.clone.1 | convolution fusion | flops 51118080 | bytes 3145920 | tf_op jit(solution)/shard_map/while/body/eval_jaxpr/pik,pkj->pij/dot_general | solution.py:26
  150.1 3.1 %copy.33 = f32[96,64,64]{0,2,1:T(8,128)S(1)} copy(f32[96,64,64]{2,1,0:T(8,128)} %fusion.36) | data formatting | bytes 3145728 | tf_op jit(solution)/shard_map/while/body/eval_jaxpr/pik,pkj->pij/dot_general | solution.py:26
  153.2 1.7 copy.34
  154.9 3.7 %scatter_fusion.1 = f32[32,4096]{1,0:T(8,128)S(1)} fusion(f32[32,4096]{1,0:T(8,128)S(1)} %get-tuple-element.240, s32[96]{0:T(128)S(1)} %fusion.35, f32[96,4096]{1,0:T(8,128)} %copy.34), kind=kCustom, calls=%fused_computation.5.clone.1 | custom fusion | flops 393216 | bytes 4718976 | tf_op jit(solution)/shard_map/while/body/eval_jaxpr/scatter-add | solution.py:29
  159.5 1.9 %gather_fusion.3 = bf16[96,64,64]{2,1,0:T(8,128)(2,1)} fusion(bf16[24,64,64]{2,1,0:T(8,128)(2,1)S(1)} %get-tuple-element.251, s32[1024]{0:T(1024)S(1)} %get-tuple-element.200), kind=kCustom, calls=%fused_computation.2.clone.clone.1 | custom fusion | bytes 1573248 | tf_op jit(solution)/shard_map/while/body/eval_jaxpr/jit(_take)/gather | solution.py:24
  161.4 3.7 %fusion.36 = f32[96,64,64]{2,1,0:T(8,128)} fusion(bf16[96,64,64]{2,1,0:T(8,128)(2,1)S(1)} %gather_fusion.2, bf16[96,64,64]{2,1,0:T(8,128)(2,1)} %gather_fusion.3, pred[96]{0:T(512)(128)(4,1)S(1)} %get-tuple-element.201, pred[96]{0:T(512)(128)(4,1)S(1)} %get-tuple-element.202), kind=kOutput, calls=%fused_computation.25.clone.1 | convolution fusion | flops 51118080 | bytes 3145920 | tf_op jit(solution)/shard_map/while/body/eval_jaxpr/pik,pkj->pij/dot_general | solution.py:26
  165.2 3.1 %copy.33 = f32[96,64,64]{0,2,1:T(8,128)S(1)} copy(f32[96,64,64]{2,1,0:T(8,128)} %fusion.36) | data formatting | bytes 3145728 | tf_op jit(solution)/shard_map/while/body/eval_jaxpr/pik,pkj->pij/dot_general | solution.py:26
  168.2 1.7 copy.34
  170.0 3.7 %scatter_fusion.1 = f32[32,4096]{1,0:T(8,128)S(1)} fusion(f32[32,4096]{1,0:T(8,128)S(1)} %get-tuple-element.240, s32[96]{0:T(128)S(1)} %fusion.35, f32[96,4096]{1,0:T(8,128)} %copy.34), kind=kCustom, calls=%fused_computation.5.clone.1 | custom fusion | flops 393216 | bytes 4718976 | tf_op jit(solution)/shard_map/while/body/eval_jaxpr/scatter-add | solution.py:29
  (58 shorter events, 11.0 us)
Async XLA Ops:
  0.6 110.0 %collective-permute-start = (bf16[1,1,24,4096]{3,2,1,0:T(8,128)(2,1)}, bf16[1,1,24,4096]{3,2,1,0:T(8,128)(2,1)}, u32[]{:S(2)}, u32[]{:S(2)}) collective-permute-start(bf16[1,1,24,4096]{3,2,1,0:T(8,128)(2,1)} %param.9), channel_id=1, source_target_pairs={{1,0},{2,1},{3,2},{4,3},{5,4},{6,5},{7,6},{0,7},{9,8},{10,9},{11,1... | collective-permute-start | bytes 589832 | tf_op jit(solution)/shard_map/ppermute | solution.py:15
  6.7 105.3 %collective-permute-start.1 = (bf16[1,1,24,4096]{3,2,1,0:T(8,128)(2,1)}, bf16[1,1,24,4096]{3,2,1,0:T(8,128)(2,1)}, u32[]{:S(2)}, u32[]{:S(2)}) collective-permute-start(bf16[1,1,24,4096]{3,2,1,0:T(8,128)(2,1)} %param.10), channel_id=1, source_target_pairs={{8,0},{16,8},{24,16},{0,24},{9,1},{17,9},{25,17},{1,25},{10,2},{18... | collective-permute-start | bytes 589832 | tf_op jit(solution)/shard_map/ppermute | solution.py:15
  113.4 0.9 copy-start
  124.7 3.7 %copy-start.1 = (bf16[24,64,64]{2,1,0:T(8,128)(2,1)S(1)}, bf16[24,64,64]{2,1,0:T(8,128)(2,1)}, u32[]{:S(2)}) copy-start(bf16[24,64,64]{2,1,0:T(8,128)(2,1)} %copy-done) | copy-start | bytes 589828 | tf_op jit(solution)/shard_map/while
  128.4 0.9 copy-start
  139.8 3.7 %copy-start.1 = (bf16[24,64,64]{2,1,0:T(8,128)(2,1)S(1)}, bf16[24,64,64]{2,1,0:T(8,128)(2,1)}, u32[]{:S(2)}) copy-start(bf16[24,64,64]{2,1,0:T(8,128)(2,1)} %copy-done) | copy-start | bytes 589828 | tf_op jit(solution)/shard_map/while
  143.5 0.9 copy-start
  154.9 3.7 %copy-start.1 = (bf16[24,64,64]{2,1,0:T(8,128)(2,1)S(1)}, bf16[24,64,64]{2,1,0:T(8,128)(2,1)}, u32[]{:S(2)}) copy-start(bf16[24,64,64]{2,1,0:T(8,128)(2,1)} %copy-done) | copy-start | bytes 589828 | tf_op jit(solution)/shard_map/while
  158.6 0.9 copy-start
  170.0 3.7 %copy-start.1 = (bf16[24,64,64]{2,1,0:T(8,128)(2,1)S(1)}, bf16[24,64,64]{2,1,0:T(8,128)(2,1)}, u32[]{:S(2)}) copy-start(bf16[24,64,64]{2,1,0:T(8,128)(2,1)} %copy-done) | copy-start | bytes 589828 | tf_op jit(solution)/shard_map/while
where the time goes:
time: 177 us; the launch traced here: 176 us
  local copies, waits for them, and re-layouts  67.1 us (38%)
  blocking collectives  37.1 us (21%)
  other arithmetic  31.9 us (18%)
  matrix products  29.7 us (17%)
  starting transfers between devices  6.71 us (4%)
  between operations  2.46 us (1%)
    psum x1, blocking collectives, global_squares(): return lax.psum(local_sum, ('row', 'col')) * scale  37.1 us
    dot_general x8, matrix products, add_group(): jnp.einsum('pik,pkj->pij', left, right, preferred_element_type=jnp.float32)  29.7 us
    scatter-add x8, other arithmetic, add_group(): jax.ops.segment_sum(blocks, group[2], num_segments=NC)  29.3 us
    dot_general x8, local copies, waits for them, and re-layouts, add_group(): jnp.einsum('pik,pkj->pij', left, right, preferred_element_type=jnp.float32)  24.6 us
    gather x8, local copies, waits for them, and re-layouts, add_group(): left = jnp.take(left_all, group[0], axis=0)  15.5 us
    reshape x8, local copies, waits for them, and re-layouts, add_group(): blocks = jnp.einsum('pik,pkj->pij', left, right, preferred_element_type=j...  13.7 us
    gather x8, local copies, waits for them, and re-layouts, add_group(): right = jnp.take(right_all, group[1], axis=0)  6.8 us
    ppermute x2, starting transfers between devices, passed_along(): return lax.ppermute(block, axis, route)  6.71 us
  transfers between devices with their start and end apart: 2, of which 0 were waited for; matrix products, arithmetic and copies ran while one was open for 38% of the time, Pallas kernels for 0%

commit v1 on v0

v1 whole, which is shorter than its diff:
```python
import functools

import jax
import jax.numpy as jnp
from jax import lax
from jax.experimental import pallas as pl
from jax.experimental.pallas import tpu as pltpu
from jax.sharding import PartitionSpec as P

BS = 64
NNZ = 24
NC = 32
LANES = 128
PAIRS = BS * BS // LANES
UNROLL = 8


def passed_along(block, axis, distance):
    devices = range(lax.axis_size(axis))
    route = [((i - distance) % len(devices), i) for i in devices]
    return lax.ppermute(block, axis, route)


def norm_kernel(a_ref, out_ref):
    x = a_ref[0, 0].astype(jnp.float32)
    x = x * x
    total = x[:, :LANES]
    for t in range(1, PAIRS):
        total = total + x[:, t * LANES : (t + 1) * LANES]
    row = jnp.sum(total, axis=0, keepdims=True)
    out_ref[...] = jnp.broadcast_to(row[None], out_ref.shape)


def step_kernel(step, a_ref, b_ref, slots_ref, *rest):
    if step == 0:
        out_ref, wide, left, pairs = rest
        total = out_ref
    else:
        before_ref, out_ref, wide, left, pairs, total = rest
    low = lax.broadcasted_iota(jnp.int32, (NNZ, LANES), 1) < BS

    for t in range(PAIRS):
        wide[pl.ds(t, NNZ, stride=PAIRS), :] = a_ref[0, 0, :, t * LANES : (t + 1) * LANES].astype(jnp.float32)
    left[...] = wide[: NNZ * PAIRS, :].astype(jnp.bfloat16)

    for t in range(PAIRS):
        x = b_ref[0, 0, :, t * LANES : (t + 1) * LANES].astype(jnp.float32)
        swapped = pltpu.roll(x, BS, 1)
        wide[pl.ds(2 * t, NNZ, stride=BS), :] = jnp.where(low, x, swapped)
        wide[pl.ds(2 * t + 1, NNZ, stride=BS), :] = jnp.where(low, swapped, x)

    side = lax.broadcasted_iota(jnp.int32, (BS, LANES), 1) < BS

    def all_pairs(p, carry):
        weights = []
        for q in range(2):
            x = wide[pl.ds(pl.multiple_of((2 * p + q) * BS, BS), BS), :]
            weights.append(
                jnp.concatenate([jnp.where(side, x, 0.0), jnp.where(side, 0.0, x)], axis=0).astype(jnp.bfloat16)
            )
        result = jnp.dot(left[...], jnp.concatenate(weights, axis=1), preferred_element_type=jnp.float32)
        for q in range(2):
            pairs[pl.ds((2 * p + q) * NNZ, NNZ)] = result[:, q * LANES : (q + 1) * LANES].reshape(NNZ, PAIRS, LANES)
        return carry

    lax.fori_loop(0, NNZ // 2, all_pairs, 0)

    if step == 0:
        total[...] = jnp.zeros_like(total)
    else:
        total[...] = before_ref[...]

    count = slots_ref.shape[-1]

    def add_entries(i, carry):
        for u in range(UNROLL):
            e = i * UNROLL + u
            at = slots_ref[0, 0, step, 1, e] * NNZ + slots_ref[0, 0, step, 0, e]
            to = slots_ref[0, 0, step, 2, e]
            total[to] = total[to] + pairs[at]
        return carry

    lax.fori_loop(0, count // UNROLL, add_entries, 0)

    if step == 1:
        flat = total.reshape((NC + 1) * PAIRS, LANES)
        for t in range(PAIRS):
            out_ref[0, 0, :, t * LANES : (t + 1) * LANES] = flat[pl.ds(t, NC, stride=PAIRS), :]


VMEM = pl.BlockSpec(memory_space=pltpu.VMEM)
SMEM = pl.BlockSpec(memory_space=pltpu.SMEM)


def accumulate(step, a_blocks, b_blocks, products, before=None):
    held = jax.ShapeDtypeStruct((NC + 1, PAIRS, LANES), jnp.float32)
    scratch = [
        pltpu.VMEM((NNZ * BS, LANES), jnp.float32),
        pltpu.VMEM((NNZ * PAIRS, LANES), jnp.bfloat16),
        pltpu.VMEM((NNZ * NNZ, PAIRS, LANES), jnp.float32),
    ]
    if step == 1:
        scratch.append(pltpu.VMEM(held.shape, held.dtype))
        result = jax.ShapeDtypeStruct((1, 1, NC, BS * BS), jnp.float32)
        operands = (a_blocks, b_blocks, products, before)
    else:
        result = held
        operands = (a_blocks, b_blocks, products)
    return pl.pallas_call(
        functools.partial(step_kernel, step),
        out_shape=result,
        in_specs=[VMEM, VMEM, SMEM] + [VMEM] * step,
        out_specs=VMEM,
        scratch_shapes=scratch,
        compiler_params=pltpu.CompilerParams(vmem_limit_bytes=32 * 1024 * 1024),
        cost_estimate=pl.CostEstimate(flops=6 * 10**8, bytes_accessed=4 * 10**6, transcendentals=0),
        name=f"step_{step}",
    )(*operands)


def global_squares(a_blocks):
    count = lax.axis_size("row") * lax.axis_size("col")
    mine = pl.pallas_call(
        norm_kernel,
        out_shape=jax.ShapeDtypeStruct((count, 1, LANES), jnp.float32),
        in_specs=[VMEM],
        out_specs=VMEM,
        name="squares",
    )(a_blocks)
    everyone = lax.all_to_all(mine, ("row", "col"), 0, 0, tiled=True)
    return jnp.sum(everyone) * jnp.float32(1.0 / (count * NNZ * BS))


def per_device(a_blocks, b_blocks, products):
    a_moved = passed_along(a_blocks, "col", -1)
    b_moved = passed_along(b_blocks, "row", -1)
    norm_sq = global_squares(a_blocks)
    first = accumulate(0, a_blocks, b_blocks, products)
    product = accumulate(1, a_moved, b_moved, products, first)
    return (product, norm_sq)


def solution(mesh):
    return jax.shard_map(
        per_device,
        mesh=mesh,
        in_specs=(
            P("row", "col", None, None),
            P("row", "col", None, None),
            P("row", "col", None, None, None),
        ),
        out_specs=(P("row", "col", None, None), P()),
        check_vma=False,
    )
```

time: 177 us -> 30.6 us (0.17)
  local copies, waits for them, and re-layouts: 67.1 us -> 0.93 us
  blocking collectives: 37.1 us -> 0 us
  other arithmetic: 31.9 us -> 0.63 us
  matrix products: 29.7 us -> 0 us
  Pallas kernels: 0 us -> 16.9 us
  starting transfers between devices: 6.71 us -> 9.38 us
    psum x1 -> x0, blocking collectives: 37.1 us -> none  [global_squares(): return lax.psum(local_sum, ('row', 'col')) * scale]
    dot_general x8 -> x0, matrix products: 29.7 us -> none  [add_group(): jnp.einsum('pik,pkj->pij', left, right, preferred_element_type=jnp.float32)]
    scatter-add x8 -> x0, other arithmetic: 29.3 us -> none  [add_group(): jax.ops.segment_sum(blocks, group[2], num_segments=NC)]
    dot_general x8 -> x0, local copies, waits for them, and re-layouts: 24.6 us -> none  [add_group(): jnp.einsum('pik,pkj->pij', left, right, preferred_element_type=jnp.float32)]
    gather x16 -> x0, local copies, waits for them, and re-layouts: 22.3 us -> none  [the longest x8 15.5 us: add_group(): left = jnp.take(left_all, group[0], axis=0)]
    pallas_call x0 -> x3, Pallas kernels: none -> 16.9 us  [the longest x2 15.3 us: accumulate(): pl.pallas_call(functools.partial(step_kernel, step), out_shape=result, in...]
    reshape x8 -> x0, local copies, waits for them, and re-layouts: 13.7 us -> none  [add_group(): blocks = jnp.einsum('pik,pkj->pij', left, right, preferred_element_type=j...]
    another operation x8 -> x0, local copies, waits for them, and re-layouts: 5.55 us -> none  [the longest x2 2.66 us: accumulate(): right_all = right_tile.reshape(-1, BS, BS)]
  transfers between devices with their start and end apart: 2 -> 3, of which waited for: 0 -> 0; matrix products, arithmetic and copies ran while one was open for 38% -> 2% of each run, Pallas kernels for 0% -> 29%
where the time goes in v1:
time: 30.6 us; the launch traced here: 30.4 us
  Pallas kernels  16.9 us (55%)
  starting transfers between devices  9.38 us (31%)
  between operations  2.48 us (8%)
  local copies, waits for them, and re-layouts  0.93 us (3%)
  other arithmetic  0.63 us (2%)
    pallas_call x2, Pallas kernels, accumulate(): pl.pallas_call(functools.partial(step_kernel, step), out_shape=result, in...  15.3 us
    ppermute x2, starting transfers between devices, passed_along(): return lax.ppermute(block, axis, route)  6.71 us
    all_to_all x1, starting transfers between devices, global_squares(): everyone = lax.all_to_all(mine, ('row', 'col'), 0, 0, tiled=True)  2.68 us
    pallas_call x1, Pallas kernels, global_squares(): pl.pallas_call(norm_kernel, out_shape=jax.ShapeDtypeStruct((count, 1, LAN...  1.59 us
    unnamed x7, local copies, waits for them, and re-layouts  0.93 us
    reduce_sum x1, other arithmetic, global_squares(): return jnp.sum(everyone) * jnp.float32(1.0 / (count * NNZ * BS))  0.63 us
  transfers between devices with their start and end apart: 3, of which 0 were waited for; matrix products, arithmetic and copies ran while one was open for 2% of the time, Pallas kernels for 29%

profile of v1, /device:TPU:0, one launch (start us, length us, event | category | flops | bytes accessed | tf_op | source)
XLA Modules:
  0.0 30.4 jit_solution(1707572110295693880)
XLA Ops:
  0.6 0.0 copy-start
  0.6 6.1 %collective-permute-start = (bf16[1,1,24,4096]{3,2,1,0:T(8,128)(2,1)}, bf16[1,1,24,4096]{3,2,1,0:T(8,128)(2,1)S(1)}, u32[]{:S(2)}, u32[]{:S(2)}) collective-permute-start(bf16[1,1,24,4096]{3,2,1,0:T(8,128)(2,1)} %a_ref.3), channel_id=1, source_target_pairs={{1,0},{2,1},{3,2},{4,3},{5,4},{6,5},{7,6},{0,7},{9,8},{10,9},{11,1... | collective-permute-start | bytes 589832 | tf_op jit(solution)/shard_map/ppermute | solution.py:21
  6.7 0.7 %collective-permute-start.1 = (bf16[1,1,24,4096]{3,2,1,0:T(8,128)(2,1)}, bf16[1,1,24,4096]{3,2,1,0:T(8,128)(2,1)S(1)}, u32[]{:S(2)}, u32[]{:S(2)}) collective-permute-start(bf16[1,1,24,4096]{3,2,1,0:T(8,128)(2,1)} %b_ref.1), channel_id=1, source_target_pairs={{8,0},{16,8},{24,16},{0,24},{9,1},{17,9},{25,17},{1,25},{10,2},{18... | collective-permute-start | bytes 589832 | tf_op jit(solution)/shard_map/ppermute | solution.py:21
  7.3 1.6 %squares.1 = f32[32,1,128]{2,1,0:T(1,128)} custom-call(bf16[1,1,24,4096]{3,2,1,0:T(8,128)(2,1)} %a_ref.3), custom_call_target="tpu_custom_call" | custom-call | tf_op jit(solution)/shard_map/squares/pallas_call | solution.py:123
  8.9 0.0 copy-start.2
  8.9 2.7 %all-to-all-start = ((f32[32,1,128]{2,1,0:T(1,128)}), f32[32,1,128]{2,1,0:T(1,128)S(1)}, u32[]{:S(2)}, u32[]{:S(2)}) async-start(f32[32,1,128]{2,1,0:T(1,128)} %squares.1), calls=%async_computation | async-start | bytes 32768 | tf_op jit(solution)/shard_map/all_to_all | solution.py:130
  11.6 0.0 copy-done.2
  11.6 0.0 copy-done
  11.7 0.0 copy-start.1
  11.7 0.9 %copy-done.1 = bf16[1,1,24,4096]{3,2,1,0:T(8,128)(2,1)S(1)} copy-done((bf16[1,1,24,4096]{3,2,1,0:T(8,128)(2,1)S(1)}, bf16[1,1,24,4096]{3,2,1,0:T(8,128)(2,1)}, u32[]{:S(2)}) %copy-start.1) | copy-done | bytes 196632
  12.6 7.1 %step_0.1.rest_0_ = f32[33,32,128]{2,1,0:T(8,128)S(1)} custom-call(bf16[1,1,24,4096]{3,2,1,0:T(8,128)(2,1)S(1)} %copy-done, bf16[1,1,24,4096]{3,2,1,0:T(8,128)(2,1)S(1)} %copy-done.1, s32[1,1,2,3,384]{4,3,2,1,0:T(4,128)S(1)} %copy.6.slots_ref), custom_call_target="tpu_custom_call" | custom-call | flops 600000000 | bytes 4000000 | tf_op jit(solution)/shard_map/step_0/pallas_call | solution.py:109
  19.7 0.0 all-to-all-done
  19.7 0.6 %reduce_sum.9 = f32[]{:T(128)} reduce(f32[32,1,128]{2,1,0:T(1,128)S(1)} %all-to-all-done, f32[]{:T(128)} %constant.0.clone.1), dimensions={0,1,2}, to_apply=%region_0.0 | reduce | flops 4095 | bytes 16392 | tf_op jit(solution)/shard_map/reduce_sum | solution.py:131
  21.0 0.0 collective-permute-done.a_ref
  21.0 0.0 collective-permute-done.1.b_ref
  21.0 8.2 %step_1.1 = f32[1,1,32,4096]{3,2,1,0:T(8,128)} custom-call(bf16[1,1,24,4096]{3,2,1,0:T(8,128)(2,1)S(1)} %collective-permute-done.a_ref, bf16[1,1,24,4096]{3,2,1,0:T(8,128)(2,1)S(1)} %collective-permute-done.1.b_ref, s32[1,1,2,3,384]{4,3,2,1,0:T(4,128)S(1)} %copy.6.slots_ref, f32[33,32,128]{2,1,0:T(8,128)S(1)} %step_0.1.rest_0_), custom_call_target="tpu_custom_call" | custom-call | flops 600000000 | bytes 4000000 | tf_op jit(solution)/shard_map/step_1/pallas_call | solution.py:109
  (1 shorter events, 0.0 us)
Async XLA Ops:
  0.6 11.0 %copy-start = (bf16[1,1,24,4096]{3,2,1,0:T(8,128)(2,1)S(1)}, bf16[1,1,24,4096]{3,2,1,0:T(8,128)(2,1)}, u32[]{:S(2)}) copy-start(bf16[1,1,24,4096]{3,2,1,0:T(8,128)(2,1)} %a_ref.3) | copy-start | bytes 589828
  0.6 20.4 %collective-permute-start = (bf16[1,1,24,4096]{3,2,1,0:T(8,128)(2,1)}, bf16[1,1,24,4096]{3,2,1,0:T(8,128)(2,1)S(1)}, u32[]{:S(2)}, u32[]{:S(2)}) collective-permute-start(bf16[1,1,24,4096]{3,2,1,0:T(8,128)(2,1)} %a_ref.3), channel_id=1, source_target_pairs={{1,0},{2,1},{3,2},{4,3},{5,4},{6,5},{7,6},{0,7},{9,8},{10,9},{11,1... | collective-permute-start | bytes 589832 | tf_op jit(solution)/shard_map/ppermute | solution.py:21
  6.7 14.3 %collective-permute-start.1 = (bf16[1,1,24,4096]{3,2,1,0:T(8,128)(2,1)}, bf16[1,1,24,4096]{3,2,1,0:T(8,128)(2,1)S(1)}, u32[]{:S(2)}, u32[]{:S(2)}) collective-permute-start(bf16[1,1,24,4096]{3,2,1,0:T(8,128)(2,1)} %b_ref.1), channel_id=1, source_target_pairs={{8,0},{16,8},{24,16},{0,24},{9,1},{17,9},{25,17},{1,25},{10,2},{18... | collective-permute-start | bytes 589832 | tf_op jit(solution)/shard_map/ppermute | solution.py:21
  8.9 2.7 %copy-start.2 = (s32[1,1,2,3,384]{4,2,3,1,0:T(2,128)S(1)}, s32[1,1,2,3,384]{4,2,3,1,0:T(2,128)}, u32[]{:S(2)}) copy-start(s32[1,1,2,3,384]{4,2,3,1,0:T(2,128)} %param.5) | copy-start | bytes 27652
  8.9 10.8 %all-to-all-start = ((f32[32,1,128]{2,1,0:T(1,128)}), f32[32,1,128]{2,1,0:T(1,128)S(1)}, u32[]{:S(2)}, u32[]{:S(2)}) async-start(f32[32,1,128]{2,1,0:T(1,128)} %squares.1), calls=%async_computation | async-start | bytes 32768 | tf_op jit(solution)/shard_map/all_to_all | solution.py:130
  11.7 0.9 %copy-start.1 = (bf16[1,1,24,4096]{3,2,1,0:T(8,128)(2,1)S(1)}, bf16[1,1,24,4096]{3,2,1,0:T(8,128)(2,1)}, u32[]{:S(2)}) copy-start(bf16[1,1,24,4096]{3,2,1,0:T(8,128)(2,1)} %b_ref.1) | copy-start | bytes 589828

commit v2 on v1

v2 whole, which is shorter than its diff:
```python
import functools

import jax
import jax.numpy as jnp
from jax import lax
from jax.experimental import pallas as pl
from jax.experimental.pallas import tpu as pltpu
from jax.sharding import PartitionSpec as P

BS = 64
NNZ = 24
NC = 32
LANES = 128
PAIRS = BS * BS // LANES
UNROLL = 16
TOTALS = 4
SHIFT = 11


def passed_along(block, axis, distance):
    devices = range(lax.axis_size(axis))
    route = [((i - distance) % len(devices), i) for i in devices]
    return lax.ppermute(block, axis, route)


def norm_kernel(a_ref, out_ref):
    x = a_ref[0, 0].astype(jnp.float32)
    x = x * x
    total = x[:, :LANES]
    for t in range(1, PAIRS):
        total = total + x[:, t * LANES : (t + 1) * LANES]
    row = jnp.sum(total, axis=0, keepdims=True)
    out_ref[...] = jnp.broadcast_to(row[None], out_ref.shape)


def step_kernel(step, a_ref, b_ref, slots_ref, *rest):
    if step == 0:
        out_ref, listed, places, wide, left, pairs, *totals, sem = rest
    else:
        before_ref, out_ref, listed, places, wide, left, pairs, *totals, sem = rest

    slots = slots_ref[0, 0, step]
    listed[...] = ((slots[1:2] * NNZ + slots[0:1]) * (PAIRS << SHIFT)) + slots[2:3] * PAIRS
    copy = pltpu.make_async_copy(listed, places, sem)
    copy.start()

    for t in range(PAIRS):
        wide[pl.ds(t, NNZ, stride=PAIRS), :] = a_ref[0, 0, :, t * LANES : (t + 1) * LANES].astype(jnp.float32)
    left[...] = wide[: NNZ * PAIRS, :].astype(jnp.bfloat16)

    low = lax.broadcasted_iota(jnp.int32, (NNZ, LANES), 1) < BS
    for t in range(PAIRS):
        x = b_ref[0, 0, :, t * LANES : (t + 1) * LANES].astype(jnp.float32)
        swapped = pltpu.roll(x, BS, 1)
        wide[pl.ds(2 * t, NNZ, stride=BS), :] = jnp.where(low, x, swapped)
        wide[pl.ds(2 * t + 1, NNZ, stride=BS), :] = jnp.where(low, swapped, x)

    for total in totals:
        total[...] = jnp.zeros_like(total)
    if step == 1:
        totals[0][...] = before_ref[...]

    side = lax.broadcasted_iota(jnp.int32, (BS, LANES), 1) < BS
    for p in range(NNZ // 2):
        weights = []
        for r in (2 * p, 2 * p + 1):
            x = wide[r * BS : (r + 1) * BS, :]
            weights.append(
                jnp.concatenate([jnp.where(side, x, 0.0), jnp.where(side, 0.0, x)], axis=0).astype(jnp.bfloat16)
            )
        result = jnp.dot(left[...], jnp.concatenate(weights, axis=1), preferred_element_type=jnp.float32)
        rows = NNZ * PAIRS
        for q in range(2):
            pairs[(2 * p + q) * rows : (2 * p + q + 1) * rows, :] = result[:, q * LANES : (q + 1) * LANES]

    copy.wait()

    def add_entries(i, carry):
        for u in range(UNROLL):
            place = places[0, i * UNROLL + u]
            at = pl.multiple_of(lax.shift_right_logical(place, SHIFT), PAIRS)
            to = pl.multiple_of(place & ((1 << SHIFT) - 1), PAIRS)
            total = totals[u % len(totals)]
            total[pl.ds(to, PAIRS), :] = total[pl.ds(to, PAIRS), :] + pairs[pl.ds(at, PAIRS), :]
        return carry

    lax.fori_loop(0, places.shape[1] // UNROLL, add_entries, 0)

    if step == 0:
        rows = out_ref.shape[0]
        out_ref[...] = (totals[0][:rows] + totals[1][:rows]) + (totals[2][:rows] + totals[3][:rows])
    else:
        for t in range(PAIRS):
            row = [total[pl.ds(t, NC, stride=PAIRS), :] for total in totals]
            out_ref[0, 0, :, t * LANES : (t + 1) * LANES] = (row[0] + row[1]) + (row[2] + row[3])


VMEM = pl.BlockSpec(memory_space=pltpu.VMEM)


def accumulate(step, a_blocks, b_blocks, products, before=None):
    held = jax.ShapeDtypeStruct(((NC + 1) * PAIRS, LANES), jnp.float32)
    count = products.shape[-1]
    if step == 1:
        result = jax.ShapeDtypeStruct((1, 1, NC, BS * BS), jnp.float32)
        operands = (a_blocks, b_blocks, products, before)
    else:
        result = held
        operands = (a_blocks, b_blocks, products)
    return pl.pallas_call(
        functools.partial(step_kernel, step),
        out_shape=result,
        in_specs=[VMEM] * len(operands),
        out_specs=VMEM,
        scratch_shapes=[
            pltpu.VMEM((1, count), jnp.int32),
            pltpu.SMEM((1, count), jnp.int32),
            pltpu.VMEM((NNZ * BS, LANES), jnp.float32),
            pltpu.VMEM((NNZ * PAIRS, LANES), jnp.bfloat16),
            pltpu.VMEM((NNZ * NNZ * PAIRS, LANES), jnp.float32),
        ]
        + [pltpu.VMEM(held.shape, held.dtype)] * TOTALS
        + [pltpu.SemaphoreType.DMA],
        compiler_params=pltpu.CompilerParams(vmem_limit_bytes=32 * 1024 * 1024),
        cost_estimate=pl.CostEstimate(flops=6 * 10**8, bytes_accessed=4 * 10**6, transcendentals=0),
        name=f"step_{step}",
    )(*operands)


def global_squares(a_blocks):
    count = lax.axis_size("row") * lax.axis_size("col")
    mine = pl.pallas_call(
        norm_kernel,
        out_shape=jax.ShapeDtypeStruct((count, 1, LANES), jnp.float32),
        in_specs=[VMEM],
        out_specs=VMEM,
        name="squares",
    )(a_blocks)
    everyone = lax.all_to_all(mine, ("row", "col"), 0, 0, tiled=True)
    return jnp.sum(everyone * jnp.float32(1.0 / (count * NNZ * BS)))


def per_device(a_blocks, b_blocks, products):
    a_moved = passed_along(a_blocks, "col", -1)
    b_moved = passed_along(b_blocks, "row", -1)
    norm_sq = global_squares(a_blocks)
    first = accumulate(0, a_blocks, b_blocks, products)
    product = accumulate(1, a_moved, b_moved, products, first)
    return (product, norm_sq)


def solution(mesh):
    return jax.shard_map(
        per_device,
        mesh=mesh,
        in_specs=(
            P("row", "col", None, None),
            P("row", "col", None, None),
            P("row", "col", None, None, None),
        ),
        out_specs=(P("row", "col", None, None), P()),
        check_vma=False,
    )
```

time: 30.6 us -> 25.3 us (0.83)
  Pallas kernels: 16.9 us -> 10.9 us
  waiting for transfers between devices: 0.01 us -> 2.55 us
  between operations: 2.48 us -> 0.69 us
    pallas_call x2, Pallas kernels: 15.3 us -> 9.34 us  [accumulate(): pl.pallas_call(functools.partial(step_kernel, step), out_shape=result, in...]
    all_to_all x1, waiting for transfers between devices: 0.01 us -> 2.55 us  [global_squares(): everyone = lax.all_to_all(mine, ('row', 'col'), 0, 0, tiled=True)]
  transfers between devices with their start and end apart: 3 -> 3, of which waited for: 0 -> 1; matrix products, arithmetic and copies ran while one was open for 2% -> 3% of each run, Pallas kernels for 29% -> 20%
where the time goes in v2:
time: 25.3 us; the launch traced here: 25.1 us
  Pallas kernels  10.9 us (43%)
  starting transfers between devices  9.38 us (37%)
  waiting for transfers between devices  2.55 us (10%)
  local copies, waits for them, and re-layouts  0.93 us (4%)
  between operations  0.69 us (3%)
  other arithmetic  0.63 us (2%)
    pallas_call x2, Pallas kernels, accumulate(): pl.pallas_call(functools.partial(step_kernel, step), out_shape=result, in...  9.34 us
    ppermute x2, starting transfers between devices, passed_along(): return lax.ppermute(block, axis, route)  6.71 us
    all_to_all x1, starting transfers between devices, global_squares(): everyone = lax.all_to_all(mine, ('row', 'col'), 0, 0, tiled=True)  2.68 us
    all_to_all x1, waiting for transfers between devices, global_squares(): everyone = lax.all_to_all(mine, ('row', 'col'), 0, 0, tiled=True)  2.55 us
    pallas_call x1, Pallas kernels, global_squares(): pl.pallas_call(norm_kernel, out_shape=jax.ShapeDtypeStruct((count, 1, LAN...  1.59 us
    unnamed x7, local copies, waits for them, and re-layouts  0.93 us
    reduce_sum x1, other arithmetic, global_squares(): return jnp.sum(everyone * jnp.float32(1.0 / (count * NNZ * BS)))  0.63 us
  transfers between devices with their start and end apart: 3, of which 1 were waited for; matrix products, arithmetic and copies ran while one was open for 3% of the time, Pallas kernels for 20%

profile of v2, /device:TPU:0, one launch (start us, length us, event | category | flops | bytes accessed | tf_op | source)
XLA Modules:
  0.0 25.1 jit_solution(3309125002069555096)
XLA Ops:
  0.6 0.0 copy-start
  0.6 6.1 %collective-permute-start = (bf16[1,1,24,4096]{3,2,1,0:T(8,128)(2,1)}, bf16[1,1,24,4096]{3,2,1,0:T(8,128)(2,1)S(1)}, u32[]{:S(2)}, u32[]{:S(2)}) collective-permute-start(bf16[1,1,24,4096]{3,2,1,0:T(8,128)(2,1)} %a_ref.3), channel_id=1, source_target_pairs={{1,0},{2,1},{3,2},{4,3},{5,4},{6,5},{7,6},{0,7},{9,8},{10,9},{11,1... | collective-permute-start | bytes 589832 | tf_op jit(solution)/shard_map/ppermute | solution.py:23
  6.7 0.7 %collective-permute-start.1 = (bf16[1,1,24,4096]{3,2,1,0:T(8,128)(2,1)}, bf16[1,1,24,4096]{3,2,1,0:T(8,128)(2,1)S(1)}, u32[]{:S(2)}, u32[]{:S(2)}) collective-permute-start(bf16[1,1,24,4096]{3,2,1,0:T(8,128)(2,1)} %b_ref.1), channel_id=1, source_target_pairs={{8,0},{16,8},{24,16},{0,24},{9,1},{17,9},{25,17},{1,25},{10,2},{18... | collective-permute-start | bytes 589832 | tf_op jit(solution)/shard_map/ppermute | solution.py:23
  7.3 1.6 %squares.1 = f32[32,1,128]{2,1,0:T(1,128)} custom-call(bf16[1,1,24,4096]{3,2,1,0:T(8,128)(2,1)} %a_ref.3), custom_call_target="tpu_custom_call" | custom-call | tf_op jit(solution)/shard_map/squares/pallas_call | solution.py:132
  8.9 0.0 copy-start.2
  8.9 2.7 %all-to-all-start = ((f32[32,1,128]{2,1,0:T(1,128)}), f32[32,1,128]{2,1,0:T(1,128)S(1)}, u32[]{:S(2)}, u32[]{:S(2)}) async-start(f32[32,1,128]{2,1,0:T(1,128)} %squares.1), calls=%async_computation | async-start | bytes 32768 | tf_op jit(solution)/shard_map/all_to_all | solution.py:139
  11.6 0.0 copy-done.2
  11.6 0.0 copy-done
  11.7 0.0 copy-start.1
  11.7 0.9 %copy-done.1 = bf16[1,1,24,4096]{3,2,1,0:T(8,128)(2,1)S(1)} copy-done((bf16[1,1,24,4096]{3,2,1,0:T(8,128)(2,1)S(1)}, bf16[1,1,24,4096]{3,2,1,0:T(8,128)(2,1)}, u32[]{:S(2)}) %copy-start.1) | copy-done | bytes 196632
  12.6 3.5 %step_0.1.rest_0_ = f32[1056,128]{1,0:T(8,128)S(1)} custom-call(bf16[1,1,24,4096]{3,2,1,0:T(8,128)(2,1)S(1)} %copy-done, bf16[1,1,24,4096]{3,2,1,0:T(8,128)(2,1)S(1)} %copy-done.1, s32[1,1,2,3,384]{4,3,2,1,0:T(4,128)S(1)} %copy.6.slots_ref), custom_call_target="tpu_custom_call" | custom-call | flops 600000000 | bytes 4000000 | tf_op jit(solution)/shard_map/step_0/pallas_call | solution.py:110
  16.1 2.5 %all-to-all-done = f32[32,1,128]{2,1,0:T(1,128)S(1)} async-done(((f32[32,1,128]{2,1,0:T(1,128)}), f32[32,1,128]{2,1,0:T(1,128)S(1)}, u32[]{:S(2)}, u32[]{:S(2)}) %all-to-all-start) | async-done | bytes 16416 | tf_op jit(solution)/shard_map/all_to_all | solution.py:139
  18.7 0.6 %multiply_reduce_fusion = f32[]{:T(128)} fusion(f32[32,1,128]{2,1,0:T(1,128)S(1)} %all-to-all-done), kind=kLoop, calls=%fused_computation | loop fusion | flops 8191 | bytes 16388 | tf_op jit(solution)/shard_map/reduce_sum | solution.py:140
  19.3 0.0 collective-permute-done.a_ref
  19.3 0.0 collective-permute-done.1.b_ref
  19.3 5.8 %step_1.1 = f32[1,1,32,4096]{3,2,1,0:T(8,128)} custom-call(bf16[1,1,24,4096]{3,2,1,0:T(8,128)(2,1)S(1)} %collective-permute-done.a_ref, bf16[1,1,24,4096]{3,2,1,0:T(8,128)(2,1)S(1)} %collective-permute-done.1.b_ref, s32[1,1,2,3,384]{4,3,2,1,0:T(4,128)S(1)} %copy.6.slots_ref, f32[1056,128]{1,0:T(8,128)S(1)} %step_0.1.rest_0_), custom_call_target="tpu_custom_call" | custom-call | flops 600000000 | bytes 4000000 | tf_op jit(solution)/shard_map/step_1/pallas_call | solution.py:110
  (1 shorter events, 0.0 us)
Async XLA Ops:
  0.6 11.0 %copy-start = (bf16[1,1,24,4096]{3,2,1,0:T(8,128)(2,1)S(1)}, bf16[1,1,24,4096]{3,2,1,0:T(8,128)(2,1)}, u32[]{:S(2)}) copy-start(bf16[1,1,24,4096]{3,2,1,0:T(8,128)(2,1)} %a_ref.3) | copy-start | bytes 589828
  0.6 18.7 %collective-permute-start = (bf16[1,1,24,4096]{3,2,1,0:T(8,128)(2,1)}, bf16[1,1,24,4096]{3,2,1,0:T(8,128)(2,1)S(1)}, u32[]{:S(2)}, u32[]{:S(2)}) collective-permute-start(bf16[1,1,24,4096]{3,2,1,0:T(8,128)(2,1)} %a_ref.3), channel_id=1, source_target_pairs={{1,0},{2,1},{3,2},{4,3},{5,4},{6,5},{7,6},{0,7},{9,8},{10,9},{11,1... | collective-permute-start | bytes 589832 | tf_op jit(solution)/shard_map/ppermute | solution.py:23
  6.7 12.6 %collective-permute-start.1 = (bf16[1,1,24,4096]{3,2,1,0:T(8,128)(2,1)}, bf16[1,1,24,4096]{3,2,1,0:T(8,128)(2,1)S(1)}, u32[]{:S(2)}, u32[]{:S(2)}) collective-permute-start(bf16[1,1,24,4096]{3,2,1,0:T(8,128)(2,1)} %b_ref.1), channel_id=1, source_target_pairs={{8,0},{16,8},{24,16},{0,24},{9,1},{17,9},{25,17},{1,25},{10,2},{18... | collective-permute-start | bytes 589832 | tf_op jit(solution)/shard_map/ppermute | solution.py:23
  8.9 2.7 %copy-start.2 = (s32[1,1,2,3,384]{4,2,3,1,0:T(2,128)S(1)}, s32[1,1,2,3,384]{4,2,3,1,0:T(2,128)}, u32[]{:S(2)}) copy-start(s32[1,1,2,3,384]{4,2,3,1,0:T(2,128)} %param.5) | copy-start | bytes 27652
  8.9 9.7 %all-to-all-start = ((f32[32,1,128]{2,1,0:T(1,128)}), f32[32,1,128]{2,1,0:T(1,128)S(1)}, u32[]{:S(2)}, u32[]{:S(2)}) async-start(f32[32,1,128]{2,1,0:T(1,128)} %squares.1), calls=%async_computation | async-start | bytes 32768 | tf_op jit(solution)/shard_map/all_to_all | solution.py:139
  11.7 0.9 %copy-start.1 = (bf16[1,1,24,4096]{3,2,1,0:T(8,128)(2,1)S(1)}, bf16[1,1,24,4096]{3,2,1,0:T(8,128)(2,1)}, u32[]{:S(2)}) copy-start(bf16[1,1,24,4096]{3,2,1,0:T(8,128)(2,1)} %b_ref.1) | copy-start | bytes 589828

commit v3 on v2

v3 whole, which is shorter than its diff:
```python
import jax
import jax.numpy as jnp
from jax import lax
from jax.experimental import pallas as pl
from jax.experimental.pallas import tpu as pltpu
from jax.sharding import PartitionSpec as P

BS = 64
NNZ = 24
NC = 32
LANES = 128
PAIRS = BS * BS // LANES
PAD = 8
APART = PAIRS + PAD
UNROLL = 16
TOTALS = 4
SHIFT = 11

VMEM = pl.BlockSpec(memory_space=pltpu.VMEM)


def passed_along(block, axis, distance):
    devices = range(lax.axis_size(axis))
    route = [((i - distance) % len(devices), i) for i in devices]
    return lax.ppermute(block, axis, route)


def squares_kernel(a_ref, out_ref):
    total = jnp.zeros((NNZ, LANES), jnp.float32)
    for t in range(PAIRS):
        x = a_ref[0, 0, :, t * LANES : (t + 1) * LANES].astype(jnp.float32)
        total = total + x * x
    row = jnp.sum(total, axis=0, keepdims=True)
    out_ref[...] = jnp.broadcast_to(row[None], out_ref.shape)


def send_list(slots_ref, step, listed, place, sem):
    left_slot, right_slot, product_slot = (slots_ref[0, 0, kind, step : step + 1] for kind in range(3))
    listed[...] = (right_slot * NNZ + left_slot) * (PAIRS << SHIFT) + product_slot * APART
    copy = pltpu.make_async_copy(listed.at[0], place, sem)
    copy.start()
    return copy


def add_products(a_ref, b_ref, places, arriving, wide, left, pairs, totals):
    for t in range(PAIRS):
        wide[pl.ds(t, NNZ, stride=APART), :] = a_ref[0, 0, :, t * LANES : (t + 1) * LANES].astype(jnp.float32)
    for n in range(NNZ):
        left[n * PAIRS : (n + 1) * PAIRS, :] = wide[n * APART : n * APART + PAIRS, :].astype(jnp.bfloat16)

    low = lax.broadcasted_iota(jnp.int32, (NNZ, LANES), 1) < BS
    for t in range(PAIRS):
        x = b_ref[0, 0, :, t * LANES : (t + 1) * LANES].astype(jnp.float32)
        swapped = pltpu.roll(x, BS, 1)
        wide[pl.ds(2 * t, NNZ, stride=BS + PAD), :] = jnp.where(low, x, swapped)
        wide[pl.ds(2 * t + 1, NNZ, stride=BS + PAD), :] = jnp.where(low, swapped, x)

    side = lax.broadcasted_iota(jnp.int32, (BS, LANES), 1) < BS
    for p in range(NNZ // 2):
        weights = []
        for r in (2 * p, 2 * p + 1):
            x = wide[r * (BS + PAD) : r * (BS + PAD) + BS, :]
            weights.append(
                jnp.concatenate([jnp.where(side, x, 0.0), jnp.where(side, 0.0, x)], axis=0).astype(jnp.bfloat16)
            )
        result = jnp.dot(left[...], jnp.concatenate(weights, axis=1), preferred_element_type=jnp.float32)
        rows = NNZ * PAIRS
        for q in range(2):
            pairs[(2 * p + q) * rows : (2 * p + q + 1) * rows, :] = result[:, q * LANES : (q + 1) * LANES]

    arriving.wait()

    def add_entries(i, carry):
        for u in range(UNROLL):
            place = places[i * UNROLL + u]
            at = pl.multiple_of(lax.shift_right_logical(place, SHIFT), PAIRS)
            to = pl.multiple_of(place & ((1 << SHIFT) - 1), PAD)
            total = totals[u % TOTALS]
            total[pl.ds(to, PAIRS), :] = total[pl.ds(to, PAIRS), :] + pairs[pl.ds(at, PAIRS), :]
        return carry

    lax.fori_loop(0, places.shape[0] // UNROLL, add_entries, 0)


def moved_kernel(a_ref, b_ref, slots_ref, *rest):
    totals = rest[:TOTALS]
    listed, place, wide, left, pairs, sem = rest[TOTALS:]

    copy = send_list(slots_ref, 1, listed, place, sem)
    for total in totals:
        total[...] = jnp.zeros_like(total)
    add_products(a_ref, b_ref, place, copy, wide, left, pairs, totals)


def own_kernel(a_ref, b_ref, slots_ref, *rest):
    _, out_ref, totals = rest[:TOTALS], rest[TOTALS], rest[TOTALS + 1 : 2 * TOTALS + 1]
    listed, place, wide, left, pairs, sem = rest[2 * TOTALS + 1 :]
    copy = send_list(slots_ref, 0, listed, place, sem)
    add_products(a_ref, b_ref, place, copy, wide, left, pairs, totals)

    for c in range(NC):
        rows = slice(c * APART, c * APART + PAIRS)
        totals[0][rows] = (totals[0][rows] + totals[1][rows]) + (totals[2][rows] + totals[3][rows])
    for t in range(PAIRS):
        out_ref[0, 0, :, t * LANES : (t + 1) * LANES] = totals[0][pl.ds(t, NC, stride=APART), :]


def both_products(a_blocks, b_blocks, a_moved, b_moved, products):
    count = products.shape[-1]
    slots = jnp.swapaxes(products, 2, 3)
    total = jax.ShapeDtypeStruct(((NC + 1) * APART, LANES), jnp.float32)
    work = [
        pltpu.VMEM((1, count), jnp.int32),
        pltpu.SMEM((count,), jnp.int32),
        pltpu.VMEM((NNZ * (BS + PAD), LANES), jnp.float32),
        pltpu.VMEM((NNZ * PAIRS, LANES), jnp.bfloat16),
        pltpu.VMEM((NNZ * NNZ * PAIRS, LANES), jnp.float32),
        pltpu.SemaphoreType.DMA,
    ]
    settings = dict(
        compiler_params=pltpu.CompilerParams(vmem_limit_bytes=32 * 1024 * 1024),
        cost_estimate=pl.CostEstimate(flops=6 * 10**8, bytes_accessed=4 * 10**6, transcendentals=0),
    )
    totals = pl.pallas_call(
        moved_kernel,
        out_shape=(total,) * TOTALS,
        in_specs=[VMEM] * 3,
        out_specs=(VMEM,) * TOTALS,
        scratch_shapes=work,
        name="moved",
        **settings,
    )(a_moved, b_moved, slots)
    return pl.pallas_call(
        own_kernel,
        out_shape=(jax.ShapeDtypeStruct((1, 1, NC, BS * BS), jnp.float32),) + (total,) * TOTALS,
        in_specs=[VMEM] * (3 + TOTALS),
        out_specs=(VMEM,) * (1 + TOTALS),
        scratch_shapes=work,
        input_output_aliases={3 + i: 1 + i for i in range(TOTALS)},
        name="own",
        **settings,
    )(a_blocks, b_blocks, slots, *totals)[0]


def spread_squares(a_blocks):
    count = lax.axis_size("row") * lax.axis_size("col")
    mine = pl.pallas_call(
        squares_kernel,
        out_shape=jax.ShapeDtypeStruct((count, 1, LANES), jnp.float32),
        in_specs=[VMEM],
        out_specs=VMEM,
        name="squares",
    )(a_blocks)
    everyone = lax.all_to_all(mine, ("row", "col"), 0, 0, tiled=True)
    return everyone, jnp.float32(1.0 / (count * NNZ * BS))


def per_device(a_blocks, b_blocks, products):
    a_moved = passed_along(a_blocks, "col", -1)
    b_moved = passed_along(b_blocks, "row", -1)
    everyone, scale = spread_squares(a_blocks)
    product = both_products(a_blocks, b_blocks, a_moved, b_moved, products)
    everyone, product = lax.optimization_barrier((everyone, product))
    norm_sq = jnp.sum(everyone * scale)
    return (product, norm_sq)


def solution(mesh):
    return jax.shard_map(
        per_device,
        mesh=mesh,
        in_specs=(
            P("row", "col", None, None),
            P("row", "col", None, None),
            P("row", "col", None, None, None),
        ),
        out_specs=(P("row", "col", None, None), P()),
        check_vma=False,
    )
```

time: 25.3 us -> 19.6 us (0.77)
  Pallas kernels: 10.9 us -> 8.42 us
  waiting for transfers between devices: 2.55 us -> 0.19 us
  local copies, waits for them, and re-layouts: 0.93 us -> 0.02 us
    pallas_call x3, Pallas kernels: 10.9 us -> 8.42 us  [the longest x1 3.83 us: both_products(): pl.pallas_call(own_kernel, out_shape=(jax.ShapeDtypeStruct((1, 1, NC, BS...]
    all_to_all x1, waiting for transfers between devices: 2.55 us -> 0.18 us  [spread_squares(): everyone = lax.all_to_all(mine, ('row', 'col'), 0, 0, tiled=True)]
    unnamed x7 -> x6, local copies, waits for them, and re-layouts: 0.93 us -> 0.02 us
  transfers between devices with their start and end apart: 3 -> 3, of which waited for: 1 -> 1; matrix products, arithmetic and copies ran while one was open for 3% -> 0% of each run, Pallas kernels for 20% -> 43%
where the time goes in v3:
time: 19.6 us; the launch traced here: 19.4 us
  starting transfers between devices  9.41 us (48%)
  Pallas kernels  8.42 us (43%)
  between operations  0.71 us (4%)
  other arithmetic  0.63 us (3%)
    ppermute x2, starting transfers between devices, passed_along(): return lax.ppermute(block, axis, route)  6.71 us
    pallas_call x1, Pallas kernels, both_products(): pl.pallas_call(own_kernel, out_shape=(jax.ShapeDtypeStruct((1, 1, NC, BS...  3.83 us
    pallas_call x1, Pallas kernels, both_products(): pl.pallas_call(moved_kernel, out_shape=(total,) * TOTALS, in_specs=[VMEM]...  3.01 us
    all_to_all x1, starting transfers between devices, spread_squares(): everyone = lax.all_to_all(mine, ('row', 'col'), 0, 0, tiled=True)  2.7 us
    pallas_call x1, Pallas kernels, spread_squares(): pl.pallas_call(squares_kernel, out_shape=jax.ShapeDtypeStruct((count, 1,...  1.58 us
    reduce_sum x1, other arithmetic, per_device(): norm_sq = jnp.sum(everyone * scale)  0.63 us
  transfers between devices with their start and end apart: 3, of which 1 were waited for; matrix products, arithmetic and copies ran while one was open for 0% of the time, Pallas kernels for 43%

profile of v3, /device:TPU:0, one launch (start us, length us, event | category | flops | bytes accessed | tf_op | source)
XLA Modules:
  0.0 19.4 jit_solution(13321790384621767185)
XLA Ops:
  0.6 6.1 %collective-permute-start = (bf16[1,1,24,4096]{3,2,1,0:T(8,128)(2,1)}, bf16[1,1,24,4096]{3,2,1,0:T(8,128)(2,1)S(1)}, u32[]{:S(2)}, u32[]{:S(2)}) collective-permute-start(bf16[1,1,24,4096]{3,2,1,0:T(8,128)(2,1)} %a_ref.3), channel_id=1, source_target_pairs={{1,0},{2,1},{3,2},{4,3},{5,4},{6,5},{7,6},{0,7},{9,8},{10,9},{11,1... | collective-permute-start | bytes 589832 | tf_op jit(solution)/shard_map/ppermute | solution.py:25
  6.7 0.7 %collective-permute-start.1 = (bf16[1,1,24,4096]{3,2,1,0:T(8,128)(2,1)}, bf16[1,1,24,4096]{3,2,1,0:T(8,128)(2,1)S(1)}, u32[]{:S(2)}, u32[]{:S(2)}) collective-permute-start(bf16[1,1,24,4096]{3,2,1,0:T(8,128)(2,1)} %b_ref.1), channel_id=1, source_target_pairs={{8,0},{16,8},{24,16},{0,24},{9,1},{17,9},{25,17},{1,25},{10,2},{18... | collective-permute-start | bytes 589832 | tf_op jit(solution)/shard_map/ppermute | solution.py:25
  7.3 1.6 %squares.1 = f32[32,1,128]{2,1,0:T(1,128)} custom-call(bf16[1,1,24,4096]{3,2,1,0:T(8,128)(2,1)} %a_ref.3), custom_call_target="tpu_custom_call" | custom-call | tf_op jit(solution)/shard_map/squares/pallas_call | solution.py:147
  8.9 0.0 copy-start.2
  8.9 2.7 %all-to-all-start = ((f32[32,1,128]{2,1,0:T(1,128)}), f32[32,1,128]{2,1,0:T(1,128)S(1)}, u32[]{:S(2)}, u32[]{:S(2)}) async-start(f32[32,1,128]{2,1,0:T(1,128)} %squares.1), calls=%async_computation | async-start | bytes 32768 | tf_op jit(solution)/shard_map/all_to_all | solution.py:154
  11.6 0.0 collective-permute-done.a_ref
  11.6 0.0 collective-permute-done.1.b_ref
  11.7 0.0 copy-done.2
  11.7 0.0 copy-start
  11.7 0.0 copy-start.1
  11.7 3.0 %moved.1 = (f32[1320,128]{1,0:T(8,128)S(1)}, f32[1320,128]{1,0:T(8,128)S(1)}, f32[1320,128]{1,0:T(8,128)S(1)}, f32[1320,128]{1,0:T(8,128)S(1)}) custom-call(bf16[1,1,24,4096]{3,2,1,0:T(8,128)(2,1)S(1)} %collective-permute-done.a_ref, bf16[1,1,24,4096]{3,2,1,0:T(8,128)(2,1)S(1)} %collective-permute-done.1.b_ref, s32[1,1,3,2,384]{4,3,2,1,0:T(2,128)S(1)} %bitcast.1), custom_call_target="tpu_custom_call" | custom-call | flops 600000000 | bytes 4000000 | tf_op jit(solution)/shard_map/moved/pallas_call | solution.py:124
  14.7 0.0 copy-done
  14.7 0.0 copy-done.1
  14.7 3.8 %own.1 = (f32[1,1,32,4096]{3,2,1,0:T(8,128)}, f32[1320,128]{1,0:T(8,128)S(1)}, f32[1320,128]{1,0:T(8,128)S(1)}, f32[1320,128]{1,0:T(8,128)S(1)}, f32[1320,128]{1,0:T(8,128)S(1)}) custom-call(bf16[1,1,24,4096]{3,2,1,0:T(8,128)(2,1)S(1)} %copy-done, ...), custom_call_target="tpu_custom_call", output_to_operand_aliasing={{1}: (3, {}), {2}: (4, {}), {3}: (5, {}), {4}: (6, {})} | custom-call | flops 600000000 | bytes 4000000 | tf_op jit(solution)/shard_map/own/pallas_call | solution.py:133
  18.6 0.2 all-to-all-done
  18.7 0.6 %multiply_reduce_fusion = f32[]{:T(128)} fusion(f32[32,1,128]{2,1,0:T(1,128)S(1)} %all-to-all-done), kind=kLoop, calls=%fused_computation | loop fusion | flops 8191 | bytes 16388 | tf_op jit(solution)/shard_map/reduce_sum | solution.py:164
Async XLA Ops:
  0.6 11.0 %collective-permute-start = (bf16[1,1,24,4096]{3,2,1,0:T(8,128)(2,1)}, bf16[1,1,24,4096]{3,2,1,0:T(8,128)(2,1)S(1)}, u32[]{:S(2)}, u32[]{:S(2)}) collective-permute-start(bf16[1,1,24,4096]{3,2,1,0:T(8,128)(2,1)} %a_ref.3), channel_id=1, source_target_pairs={{1,0},{2,1},{3,2},{4,3},{5,4},{6,5},{7,6},{0,7},{9,8},{10,9},{11,1... | collective-permute-start | bytes 589832 | tf_op jit(solution)/shard_map/ppermute | solution.py:25
  6.7 5.0 %collective-permute-start.1 = (bf16[1,1,24,4096]{3,2,1,0:T(8,128)(2,1)}, bf16[1,1,24,4096]{3,2,1,0:T(8,128)(2,1)S(1)}, u32[]{:S(2)}, u32[]{:S(2)}) collective-permute-start(bf16[1,1,24,4096]{3,2,1,0:T(8,128)(2,1)} %b_ref.1), channel_id=1, source_target_pairs={{8,0},{16,8},{24,16},{0,24},{9,1},{17,9},{25,17},{1,25},{10,2},{18... | collective-permute-start | bytes 589832 | tf_op jit(solution)/shard_map/ppermute | solution.py:25
  8.9 2.7 %copy-start.2 = (s32[1,1,2,3,384]{4,2,3,1,0:T(2,128)S(1)}, s32[1,1,2,3,384]{4,2,3,1,0:T(2,128)}, u32[]{:S(2)}) copy-start(s32[1,1,2,3,384]{4,2,3,1,0:T(2,128)} %param.5) | copy-start | bytes 27652
  8.9 9.8 %all-to-all-start = ((f32[32,1,128]{2,1,0:T(1,128)}), f32[32,1,128]{2,1,0:T(1,128)S(1)}, u32[]{:S(2)}, u32[]{:S(2)}) async-start(f32[32,1,128]{2,1,0:T(1,128)} %squares.1), calls=%async_computation | async-start | bytes 32768 | tf_op jit(solution)/shard_map/all_to_all | solution.py:154
  11.7 3.0 %copy-start = (bf16[1,1,24,4096]{3,2,1,0:T(8,128)(2,1)S(1)}, bf16[1,1,24,4096]{3,2,1,0:T(8,128)(2,1)}, u32[]{:S(2)}) copy-start(bf16[1,1,24,4096]{3,2,1,0:T(8,128)(2,1)} %a_ref.3) | copy-start | bytes 589828
  11.7 3.0 %copy-start.1 = (bf16[1,1,24,4096]{3,2,1,0:T(8,128)(2,1)S(1)}, bf16[1,1,24,4096]{3,2,1,0:T(8,128)(2,1)}, u32[]{:S(2)}) copy-start(bf16[1,1,24,4096]{3,2,1,0:T(8,128)(2,1)} %b_ref.1) | copy-start | bytes 589828

commit v4 on v3

--- a/solution.py
+++ b/solution.py
@@ -1,3 +1,5 @@
+import functools
+
 import jax
 import jax.numpy as jnp
 from jax import lax
@@ -15,8 +17,10 @@
 UNROLL = 16
 TOTALS = 4
 SHIFT = 11
+PREPARE_VMEM = 66450000
 
 VMEM = pl.BlockSpec(memory_space=pltpu.VMEM)
+ANY = pl.BlockSpec(memory_space=pl.ANY)
 
 
 def passed_along(block, axis, distance):
@@ -25,13 +29,27 @@
     return lax.ppermute(block, axis, route)
 
 
-def squares_kernel(a_ref, out_ref):
-    total = jnp.zeros((NNZ, LANES), jnp.float32)
-    for t in range(PAIRS):
-        x = a_ref[0, 0, :, t * LANES : (t + 1) * LANES].astype(jnp.float32)
-        total = total + x * x
-    row = jnp.sum(total, axis=0, keepdims=True)
-    out_ref[...] = jnp.broadcast_to(row[None], out_ref.shape)
+def prepare_kernel(first_column, a_ref, b_ref, *rest):
+    squares_ref, a_near, b_near, spread, a_sem, b_sem, out_sem = rest[-7:]
+    at_start = lax.axis_index("col") == 0
+
+    @pl.when(at_start if first_column else jnp.logical_not(at_start))
+    def _():
+        a_copy = pltpu.make_async_copy(a_ref, a_near, a_sem)
+        b_copy = pltpu.make_async_copy(b_ref, b_near, b_sem)
+        a_copy.start()
+        b_copy.start()
+        a_copy.wait()
+        total = jnp.zeros((NNZ, LANES), jnp.float32)
+        for t in range(PAIRS):
+            x = a_near[0, 0, :, t * LANES : (t + 1) * LANES].astype(jnp.float32)
+            total = total + x * x
+        row = jnp.sum(total, axis=0, keepdims=True)
+        spread[...] = jnp.broadcast_to(row[None], spread.shape)
+        out_copy = pltpu.make_async_copy(spread, squares_ref, out_sem)
+        out_copy.start()
+        b_copy.wait()
+        out_copy.wait()
 
 
 def send_list(slots_ref, step, listed, place, sem):
@@ -82,20 +100,19 @@
     lax.fori_loop(0, places.shape[0] // UNROLL, add_entries, 0)
 
 
-def moved_kernel(a_ref, b_ref, slots_ref, *rest):
+def own_kernel(a_ref, b_ref, slots_ref, *rest):
     totals = rest[:TOTALS]
     listed, place, wide, left, pairs, sem = rest[TOTALS:]
-
-    copy = send_list(slots_ref, 1, listed, place, sem)
+    copy = send_list(slots_ref, 0, listed, place, sem)
     for total in totals:
         total[...] = jnp.zeros_like(total)
     add_products(a_ref, b_ref, place, copy, wide, left, pairs, totals)
 
 
-def own_kernel(a_ref, b_ref, slots_ref, *rest):
+def moved_kernel(a_ref, b_ref, slots_ref, *rest):
     _, out_ref, totals = rest[:TOTALS], rest[TOTALS], rest[TOTALS + 1 : 2 * TOTALS + 1]
     listed, place, wide, left, pairs, sem = rest[2 * TOTALS + 1 :]
-    copy = send_list(slots_ref, 0, listed, place, sem)
+    copy = send_list(slots_ref, 1, listed, place, sem)
     add_products(a_ref, b_ref, place, copy, wide, left, pairs, totals)
 
     for c in range(NC):
@@ -109,59 +126,70 @@
     count = products.shape[-1]
     slots = jnp.swapaxes(products, 2, 3)
     total = jax.ShapeDtypeStruct(((NC + 1) * APART, LANES), jnp.float32)
-    work = [
-        pltpu.VMEM((1, count), jnp.int32),
-        pltpu.SMEM((count,), jnp.int32),
-        pltpu.VMEM((NNZ * (BS + PAD), LANES), jnp.float32),
-        pltpu.VMEM((NNZ * PAIRS, LANES), jnp.bfloat16),
-        pltpu.VMEM((NNZ * NNZ * PAIRS, LANES), jnp.float32),
-        pltpu.SemaphoreType.DMA,
-    ]
     settings = dict(
+        scratch_shapes=[
+            pltpu.VMEM((1, count), jnp.int32),
+            pltpu.SMEM((count,), jnp.int32),
+            pltpu.VMEM((NNZ * (BS + PAD), LANES), jnp.float32),
+            pltpu.VMEM((NNZ * PAIRS, LANES), jnp.bfloat16),
+            pltpu.VMEM((NNZ * NNZ * PAIRS, LANES), jnp.float32),
+            pltpu.SemaphoreType.DMA,
+        ],
         compiler_params=pltpu.CompilerParams(vmem_limit_bytes=32 * 1024 * 1024),
         cost_estimate=pl.CostEstimate(flops=6 * 10**8, bytes_accessed=4 * 10**6, transcendentals=0),
     )
     totals = pl.pallas_call(
-        moved_kernel,
+        own_kernel,
         out_shape=(total,) * TOTALS,
         in_specs=[VMEM] * 3,
         out_specs=(VMEM,) * TOTALS,
-        scratch_shapes=work,
-        name="moved",
+        name="own",
         **settings,
-    )(a_moved, b_moved, slots)
+    )(a_blocks, b_blocks, slots)
     return pl.pallas_call(
-        own_kernel,
+        moved_kernel,
         out_shape=(jax.ShapeDtypeStruct((1, 1, NC, BS * BS), jnp.float32),) + (total,) * TOTALS,
         in_specs=[VMEM] * (3 + TOTALS),
         out_specs=(VMEM,) * (1 + TOTALS),
-        scratch_shapes=work,
         input_output_aliases={3 + i: 1 + i for i in range(TOTALS)},
-        name="own",
+        name="moved",
         **settings,
-    )(a_blocks, b_blocks, slots, *totals)[0]
-
-
-def spread_squares(a_blocks):
+    )(a_moved, b_moved, slots, *totals)[0]
+
+
+def prepare(a_blocks, b_blocks, count, before=()):
+    first_column = not before
+    return pl.pallas_call(
+        functools.partial(prepare_kernel, first_column),
+        out_shape=(
+            jax.ShapeDtypeStruct((count, 1, LANES), jnp.float32),
+            pltpu.VMEM(a_blocks.shape, a_blocks.dtype),
+            pltpu.VMEM(b_blocks.shape, b_blocks.dtype),
+        ),
+        in_specs=[ANY, ANY] + [ANY, VMEM, VMEM][: len(before)],
+        out_specs=(ANY, VMEM, VMEM),
+        scratch_shapes=[pltpu.VMEM((count, 1, LANES), jnp.float32)] + [pltpu.SemaphoreType.DMA] * 3,
+        input_output_aliases={} if first_column else {2: 0, 3: 1, 4: 2},
+        compiler_params=pltpu.CompilerParams(vmem_limit_bytes=PREPARE_VMEM) if first_column else None,
+        name="prepare_early" if first_column else "prepare_late",
+    )(
+        pltpu.with_memory_space_constraint(a_blocks, pltpu.HBM),
+        pltpu.with_memory_space_constraint(b_blocks, pltpu.HBM),
+        *before,
+    )
+
+
+def per_device(a_blocks, b_blocks, products):
     count = lax.axis_size("row") * lax.axis_size("col")
-    mine = pl.pallas_call(
-        squares_kernel,
-        out_shape=jax.ShapeDtypeStruct((count, 1, LANES), jnp.float32),
-        in_specs=[VMEM],
-        out_specs=VMEM,
-        name="squares",
-    )(a_blocks)
-    everyone = lax.all_to_all(mine, ("row", "col"), 0, 0, tiled=True)
-    return everyone, jnp.float32(1.0 / (count * NNZ * BS))
-
-
-def per_device(a_blocks, b_blocks, products):
-    a_moved = passed_along(a_blocks, "col", -1)
+    ready = prepare(a_blocks, b_blocks, count)
+    *ready, a_after = lax.optimization_barrier((*ready, a_blocks))
+    a_moved = passed_along(a_after, "col", -1)
     b_moved = passed_along(b_blocks, "row", -1)
-    everyone, scale = spread_squares(a_blocks)
-    product = both_products(a_blocks, b_blocks, a_moved, b_moved, products)
+    squares, a_near, b_near = prepare(a_blocks, b_blocks, count, tuple(ready))
+    everyone = lax.all_to_all(squares, ("row", "col"), 0, 0, tiled=True)
+    product = both_products(a_near, b_near, a_moved, b_moved, products)
     everyone, product = lax.optimization_barrier((everyone, product))
-    norm_sq = jnp.sum(everyone * scale)
+    norm_sq = jnp.sum(everyone * jnp.float32(1.0 / (count * NNZ * BS)))
     return (product, norm_sq)
 
 

time: 19.6 us -> 18.3 us (0.934)
  starting transfers between devices: 9.41 us -> 8.04 us
    ppermute x2, starting transfers between devices: 6.71 us -> 5.46 us  [passed_along(): return lax.ppermute(block, axis, route)]
    pallas_call x3 -> x4, Pallas kernels: 8.42 us -> 8.53 us  [the longest x1 3.85 us: both_products(): pl.pallas_call(moved_kernel, out_shape=(jax.ShapeDtypeStruct((1, 1, NC, B...]
  transfers between devices with their start and end apart: 3 -> 3, of which waited for: 1 -> 1; matrix products, arithmetic and copies ran while one was open for 0% -> 0% of each run, Pallas kernels for 43% -> 47%
where the time goes in v4:
time: 18.3 us; the launch traced here: 18.1 us
  Pallas kernels  8.53 us (47%)
  starting transfers between devices  8.04 us (44%)
  between operations  0.7 us (4%)
  other arithmetic  0.63 us (3%)
    ppermute x2, starting transfers between devices, passed_along(): return lax.ppermute(block, axis, route)  5.46 us
    pallas_call x1, Pallas kernels, both_products(): pl.pallas_call(moved_kernel, out_shape=(jax.ShapeDtypeStruct((1, 1, NC, B...  3.85 us
    pallas_call x1, Pallas kernels, both_products(): pl.pallas_call(own_kernel, out_shape=(total,) * TOTALS, in_specs=[VMEM] *...  3.05 us
    all_to_all x1, starting transfers between devices, per_device(): everyone = lax.all_to_all(squares, ('row', 'col'), 0, 0, tiled=True)  2.58 us
    pallas_call x2, Pallas kernels, prepare(): pl.pallas_call(functools.partial(prepare_kernel, first_column), out_shape...  1.63 us
    reduce_sum x1, other arithmetic, per_device(): norm_sq = jnp.sum(everyone * jnp.float32(1.0 / (count * NNZ * BS)))  0.63 us
  transfers between devices with their start and end apart: 3, of which 1 were waited for; matrix products, arithmetic and copies ran while one was open for 0% of the time, Pallas kernels for 47%

profile of v4, /device:TPU:0, one launch (start us, length us, event | category | flops | bytes accessed | tf_op | source)
XLA Modules:
  0.0 18.1 jit_solution(9602902863183325355)
XLA Ops:
  0.6 2.4 %collective-permute-start.1 = (bf16[1,1,24,4096]{3,2,1,0:T(8,128)(2,1)}, bf16[1,1,24,4096]{3,2,1,0:T(8,128)(2,1)S(1)}, u32[]{:S(2)}, u32[]{:S(2)}) collective-permute-start(bf16[1,1,24,4096]{3,2,1,0:T(8,128)(2,1)} %b_ref.3), channel_id=1, source_target_pairs={{8,0},{16,8},{24,16},{0,24},{9,1},{17,9},{25,17},{1,25},{10,2},{18... | collective-permute-start | bytes 589832 | tf_op jit(solution)/shard_map/ppermute | solution.py:29
  3.1 1.6 %prepare_early.1 = (f32[32,1,128]{2,1,0:T(1,128)}, bf16[1,1,24,4096]{3,2,1,0:T(8,128)(2,1)S(1)}, bf16[1,1,24,4096]{3,2,1,0:T(8,128)(2,1)S(1)}) custom-call(bf16[1,1,24,4096]{3,2,1,0:T(8,128)(2,1)} %a_ref.3, bf16[1,1,24,4096]{3,2,1,0:T(8,128)(2,1)} %b_ref.3), custom_call_target="tpu_custom_call" | custom-call | tf_op jit(solution)/shard_map/prepare_early/pallas_call | solution.py:162
  4.7 3.0 %collective-permute-start = (bf16[1,1,24,4096]{3,2,1,0:T(8,128)(2,1)}, bf16[1,1,24,4096]{3,2,1,0:T(8,128)(2,1)S(1)}, u32[]{:S(2)}, u32[]{:S(2)}) collective-permute-start(bf16[1,1,24,4096]{3,2,1,0:T(8,128)(2,1)} %a_ref.3), channel_id=1, source_target_pairs={{1,0},{2,1},{3,2},{4,3},{5,4},{6,5},{7,6},{0,7},{9,8},{10,9},{11,1... | collective-permute-start | bytes 589832 | tf_op jit(solution)/shard_map/ppermute | solution.py:29
  7.7 0.0 copy-start
  7.8 2.6 %all-to-all-start = ((f32[32,1,128]{2,1,0:T(1,128)}), f32[32,1,128]{2,1,0:T(1,128)S(1)}, u32[]{:S(2)}, u32[]{:S(2)}) async-start(f32[32,1,128]{2,1,0:T(1,128)} %get-tuple-element.25), calls=%async_computation | async-start | bytes 32768 | tf_op jit(solution)/shard_map/all_to_all | solution.py:189
  10.3 0.0 copy-done
  10.4 3.0 %own.1 = (f32[1320,128]{1,0:T(8,128)S(1)}, f32[1320,128]{1,0:T(8,128)S(1)}, f32[1320,128]{1,0:T(8,128)S(1)}, f32[1320,128]{1,0:T(8,128)S(1)}) custom-call(bf16[1,1,24,4096]{3,2,1,0:T(8,128)(2,1)S(1)} %get-tuple-element.27.a_ref, bf16[1,1,24,4096]{3,2,1,0:T(8,128)(2,1)S(1)} %get-tuple-element.28.b_ref, s32[1,1,3,2,384]{4,3,2,1,0:T(2,128)S(1)} %bitcast.1), custom_call_target="tpu_custom_call" | custom-call | flops 600000000 | bytes 4000000 | tf_op jit(solution)/shard_map/own/pallas_call | solution.py:141
  13.4 0.0 collective-permute-done.1.b_ref
  13.4 0.0 collective-permute-done.a_ref
  13.4 3.8 %moved.1 = (f32[1,1,32,4096]{3,2,1,0:T(8,128)}, f32[1320,128]{1,0:T(8,128)S(1)}, f32[1320,128]{1,0:T(8,128)S(1)}, f32[1320,128]{1,0:T(8,128)S(1)}, f32[1320,128]{1,0:T(8,128)S(1)}) custom-call(bf16[1,1,24,4096]{3,2,1,0:T(8,128)(2,1)S(1)} %collective-permute-done.a_ref, ...), custom_call_target="tpu_custom_call", output_to_operand_aliasing={{1}: (3, {}), {2}: (4, {}), {3}: (5, {}), {4}: (6, {})} | custom-call | flops 600000000 | bytes 4000000 | tf_op jit(solution)/shard_map/moved/pallas_call | solution.py:149
  17.3 0.2 all-to-all-done
  17.5 0.6 %multiply_reduce_fusion = f32[]{:T(128)} fusion(f32[32,1,128]{2,1,0:T(1,128)S(1)} %all-to-all-done), kind=kLoop, calls=%fused_computation | loop fusion | flops 8191 | bytes 16388 | tf_op jit(solution)/shard_map/reduce_sum | solution.py:192
  (1 shorter events, 0.0 us)
Async XLA Ops:
  0.6 12.8 %collective-permute-start.1 = (bf16[1,1,24,4096]{3,2,1,0:T(8,128)(2,1)}, bf16[1,1,24,4096]{3,2,1,0:T(8,128)(2,1)S(1)}, u32[]{:S(2)}, u32[]{:S(2)}) collective-permute-start(bf16[1,1,24,4096]{3,2,1,0:T(8,128)(2,1)} %b_ref.3), channel_id=1, source_target_pairs={{8,0},{16,8},{24,16},{0,24},{9,1},{17,9},{25,17},{1,25},{10,2},{18... | collective-permute-start | bytes 589832 | tf_op jit(solution)/shard_map/ppermute | solution.py:29
  4.7 8.7 %collective-permute-start = (bf16[1,1,24,4096]{3,2,1,0:T(8,128)(2,1)}, bf16[1,1,24,4096]{3,2,1,0:T(8,128)(2,1)S(1)}, u32[]{:S(2)}, u32[]{:S(2)}) collective-permute-start(bf16[1,1,24,4096]{3,2,1,0:T(8,128)(2,1)} %a_ref.3), channel_id=1, source_target_pairs={{1,0},{2,1},{3,2},{4,3},{5,4},{6,5},{7,6},{0,7},{9,8},{10,9},{11,1... | collective-permute-start | bytes 589832 | tf_op jit(solution)/shard_map/ppermute | solution.py:29
  7.7 2.6 %copy-start = (s32[1,1,2,3,384]{4,2,3,1,0:T(2,128)S(1)}, s32[1,1,2,3,384]{4,2,3,1,0:T(2,128)}, u32[]{:S(2)}) copy-start(s32[1,1,2,3,384]{4,2,3,1,0:T(2,128)} %param.5) | copy-start | bytes 27652
  7.8 9.7 %all-to-all-start = ((f32[32,1,128]{2,1,0:T(1,128)}), f32[32,1,128]{2,1,0:T(1,128)S(1)}, u32[]{:S(2)}, u32[]{:S(2)}) async-start(f32[32,1,128]{2,1,0:T(1,128)} %get-tuple-element.25), calls=%async_computation | async-start | bytes 32768 | tf_op jit(solution)/shard_map/all_to_all | solution.py:189

commit v5 on v4

--- a/solution.py
+++ b/solution.py
@@ -17,7 +17,8 @@
 UNROLL = 16
 TOTALS = 4
 SHIFT = 11
-PREPARE_VMEM = 66450000
+FULL_VMEM = 66900000
+SOME_VMEM = 16 * 1024 * 1024
 
 VMEM = pl.BlockSpec(memory_space=pltpu.VMEM)
 ANY = pl.BlockSpec(memory_space=pl.ANY)
@@ -29,27 +30,38 @@
     return lax.ppermute(block, axis, route)
 
 
-def prepare_kernel(first_column, a_ref, b_ref, *rest):
-    squares_ref, a_near, b_near, spread, a_sem, b_sem, out_sem = rest[-7:]
+def squares_kernel(first_column, a_ref, *rest):
+    out_ref, a_held, spread, a_sem, out_sem = rest[-5:]
     at_start = lax.axis_index("col") == 0
 
     @pl.when(at_start if first_column else jnp.logical_not(at_start))
     def _():
-        a_copy = pltpu.make_async_copy(a_ref, a_near, a_sem)
-        b_copy = pltpu.make_async_copy(b_ref, b_near, b_sem)
-        a_copy.start()
-        b_copy.start()
-        a_copy.wait()
+        held = a_ref
+        if first_column:
+            held = a_held
+            a_copy = pltpu.make_async_copy(a_ref, a_held, a_sem)
+            a_copy.start()
+            a_copy.wait()
         total = jnp.zeros((NNZ, LANES), jnp.float32)
         for t in range(PAIRS):
-            x = a_near[0, 0, :, t * LANES : (t + 1) * LANES].astype(jnp.float32)
+            x = held[0, 0, :, t * LANES : (t + 1) * LANES].astype(jnp.float32)
             total = total + x * x
         row = jnp.sum(total, axis=0, keepdims=True)
         spread[...] = jnp.broadcast_to(row[None], spread.shape)
-        out_copy = pltpu.make_async_copy(spread, squares_ref, out_sem)
+        out_copy = pltpu.make_async_copy(spread, out_ref, out_sem)
         out_copy.start()
-        b_copy.wait()
         out_copy.wait()
+
+
+def after(token, name, limit, width=LANES):
+    return pl.pallas_call(
+        lambda token_ref, out_ref: None,
+        out_shape=pltpu.HBM((8, width), jnp.float32),
+        in_specs=[ANY],
+        out_specs=ANY,
+        compiler_params=pltpu.CompilerParams(vmem_limit_bytes=limit),
+        name=name,
+    )(pltpu.with_memory_space_constraint(token, pltpu.HBM))
 
 
 def send_list(slots_ref, step, listed, place, sem):
@@ -157,36 +169,40 @@
     )(a_moved, b_moved, slots, *totals)[0]
 
 
-def prepare(a_blocks, b_blocks, count, before=()):
+def squares(a_blocks, count, before=()):
     first_column = not before
     return pl.pallas_call(
-        functools.partial(prepare_kernel, first_column),
-        out_shape=(
-            jax.ShapeDtypeStruct((count, 1, LANES), jnp.float32),
+        functools.partial(squares_kernel, first_column),
+        out_shape=pltpu.HBM((count, 1, LANES), jnp.float32),
+        in_specs=[ANY if first_column else VMEM] + [ANY] * len(before),
+        out_specs=ANY,
+        scratch_shapes=[
             pltpu.VMEM(a_blocks.shape, a_blocks.dtype),
-            pltpu.VMEM(b_blocks.shape, b_blocks.dtype),
-        ),
-        in_specs=[ANY, ANY] + [ANY, VMEM, VMEM][: len(before)],
-        out_specs=(ANY, VMEM, VMEM),
-        scratch_shapes=[pltpu.VMEM((count, 1, LANES), jnp.float32)] + [pltpu.SemaphoreType.DMA] * 3,
-        input_output_aliases={} if first_column else {2: 0, 3: 1, 4: 2},
-        compiler_params=pltpu.CompilerParams(vmem_limit_bytes=PREPARE_VMEM) if first_column else None,
-        name="prepare_early" if first_column else "prepare_late",
+            pltpu.VMEM((count, 1, LANES), jnp.float32),
+            pltpu.SemaphoreType.DMA,
+            pltpu.SemaphoreType.DMA,
+        ],
+        input_output_aliases={} if first_column else {1: 0},
+        compiler_params=pltpu.CompilerParams(vmem_limit_bytes=FULL_VMEM) if first_column else None,
+        name="squares_early" if first_column else "squares_late",
     )(
-        pltpu.with_memory_space_constraint(a_blocks, pltpu.HBM),
-        pltpu.with_memory_space_constraint(b_blocks, pltpu.HBM),
-        *before,
+        pltpu.with_memory_space_constraint(a_blocks, pltpu.HBM if first_column else pltpu.VMEM),
+        *(pltpu.with_memory_space_constraint(x, pltpu.HBM) for x in before),
     )
 
 
 def per_device(a_blocks, b_blocks, products):
     count = lax.axis_size("row") * lax.axis_size("col")
-    ready = prepare(a_blocks, b_blocks, count)
-    *ready, a_after = lax.optimization_barrier((*ready, a_blocks))
+    ready = squares(a_blocks, count)
+    first = after(after(ready, "first", FULL_VMEM), "second", FULL_VMEM)
+    first, a_after = lax.optimization_barrier((first, a_blocks))
     a_moved = passed_along(a_after, "col", -1)
-    b_moved = passed_along(b_blocks, "row", -1)
-    squares, a_near, b_near = prepare(a_blocks, b_blocks, count, tuple(ready))
-    everyone = lax.all_to_all(squares, ("row", "col"), 0, 0, tiled=True)
+    third = after(ready, "third", SOME_VMEM, 8192)
+    third, b_after = lax.optimization_barrier((third, b_blocks))
+    b_moved = passed_along(b_after, "row", -1)
+    ready = squares(a_blocks, count, (ready, first, third))
+    everyone = lax.all_to_all(ready, ("row", "col"), 0, 0, tiled=True)
+    a_near, b_near = (pltpu.with_memory_space_constraint(x, pltpu.VMEM) for x in (a_blocks, b_blocks))
     product = both_products(a_near, b_near, a_moved, b_moved, products)
     everyone, product = lax.optimization_barrier((everyone, product))
     norm_sq = jnp.sum(everyone * jnp.float32(1.0 / (count * NNZ * BS)))

time: 18.3 us -> 18 us (0.984)
  starting transfers between devices: 8.04 us -> 7.71 us
    ppermute x2, starting transfers between devices: 5.46 us -> 5.13 us  [passed_along(): return lax.ppermute(block, axis, route)]
    pallas_call x2 -> x5, Pallas kernels: 1.63 us -> 1.63 us  [the longest x2 1.63 us: squares(): pl.pallas_call(functools.partial(squares_kernel, first_column), out_shape...]
  transfers between devices with their start and end apart: 3 -> 3, of which waited for: 1 -> 1; matrix products, arithmetic and copies ran while one was open for 0% -> 0% of each run, Pallas kernels for 47% -> 39%
where the time goes in v5:
time: 18 us; the launch traced here: 17.8 us
  Pallas kernels  8.48 us (47%)
  starting transfers between devices  7.71 us (43%)
  between operations  0.73 us (4%)
  other arithmetic  0.63 us (4%)
  waiting for transfers between devices  0.21 us (1%)
    ppermute x2, starting transfers between devices, passed_along(): return lax.ppermute(block, axis, route)  5.13 us
    pallas_call x1, Pallas kernels, both_products(): pl.pallas_call(moved_kernel, out_shape=(jax.ShapeDtypeStruct((1, 1, NC, B...  3.83 us
    pallas_call x1, Pallas kernels, both_products(): pl.pallas_call(own_kernel, out_shape=(total,) * TOTALS, in_specs=[VMEM] *...  3.02 us
    all_to_all x1, starting transfers between devices, per_device(): everyone = lax.all_to_all(ready, ('row', 'col'), 0, 0, tiled=True)  2.58 us
    pallas_call x2, Pallas kernels, squares(): pl.pallas_call(functools.partial(squares_kernel, first_column), out_shape...  1.63 us
    reduce_sum x1, other arithmetic, per_device(): norm_sq = jnp.sum(everyone * jnp.float32(1.0 / (count * NNZ * BS)))  0.63 us
  transfers between devices with their start and end apart: 3, of which 1 were waited for; matrix products, arithmetic and copies ran while one was open for 0% of the time, Pallas kernels for 39%

profile of v5, /device:TPU:0, one launch (start us, length us, event | category | flops | bytes accessed | tf_op | source)
XLA Modules:
  0.0 17.8 jit_solution(4162666324207461649)
XLA Ops:
  0.6 1.6 %squares_early.1.token_ref.rest_0_ = f32[32,1,128]{2,1,0:T(1,128)} custom-call(bf16[1,1,24,4096]{3,2,1,0:T(8,128)(2,1)} %a_ref.5), custom_call_target="tpu_custom_call" | custom-call | tf_op jit(solution)/shard_map/squares_early/pallas_call | solution.py:174
  2.3 0.0 copy-start
  2.3 4.5 %collective-permute-start = (bf16[1,1,24,4096]{3,2,1,0:T(8,128)(2,1)}, bf16[1,1,24,4096]{3,2,1,0:T(8,128)(2,1)S(1)}, u32[]{:S(2)}, u32[]{:S(2)}) collective-permute-start(bf16[1,1,24,4096]{3,2,1,0:T(8,128)(2,1)} %a_ref.5), channel_id=1, source_target_pairs={{1,0},{2,1},{3,2},{4,3},{5,4},{6,5},{7,6},{0,7},{9,8},{10,9},{11,1... | collective-permute-start | bytes 589832 | tf_op jit(solution)/shard_map/ppermute | solution.py:30
  6.8 0.0 copy-start.2
  6.8 0.7 %collective-permute-start.1 = (bf16[1,1,24,4096]{3,2,1,0:T(8,128)(2,1)}, bf16[1,1,24,4096]{3,2,1,0:T(8,128)(2,1)S(1)}, u32[]{:S(2)}, u32[]{:S(2)}) collective-permute-start(bf16[1,1,24,4096]{3,2,1,0:T(8,128)(2,1)} %b_ref.1), channel_id=1, source_target_pairs={{8,0},{16,8},{24,16},{0,24},{9,1},{17,9},{25,17},{1,25},{10,2},{18... | collective-permute-start | bytes 589832 | tf_op jit(solution)/shard_map/ppermute | solution.py:30
  7.4 0.0 copy-done
  7.4 0.0 copy-start.1
  7.5 2.6 %all-to-all-start = ((f32[32,1,128]{2,1,0:T(1,128)}), f32[32,1,128]{2,1,0:T(1,128)S(1)}, u32[]{:S(2)}, u32[]{:S(2)}) async-start(f32[32,1,128]{2,1,0:T(1,128)} %squares_late.1), calls=%async_computation | async-start | bytes 32768 | tf_op jit(solution)/shard_map/all_to_all | solution.py:204
  10.0 0.0 copy-done.2
  10.1 0.0 copy-done.1
  10.1 3.0 %own.1 = (f32[1320,128]{1,0:T(8,128)S(1)}, f32[1320,128]{1,0:T(8,128)S(1)}, f32[1320,128]{1,0:T(8,128)S(1)}, f32[1320,128]{1,0:T(8,128)S(1)}) custom-call(bf16[1,1,24,4096]{3,2,1,0:T(8,128)(2,1)S(1)} %copy-done, bf16[1,1,24,4096]{3,2,1,0:T(8,128)(2,1)S(1)} %copy-done.2, s32[1,1,3,2,384]{4,3,2,1,0:T(2,128)S(1)} %bitcast.1), custom_call_target="tpu_custom_call" | custom-call | flops 600000000 | bytes 4000000 | tf_op jit(solution)/shard_map/own/pallas_call | solution.py:153
  13.1 0.0 collective-permute-done.a_ref
  13.1 0.0 collective-permute-done.1.b_ref
  13.1 3.8 %moved.1 = (f32[1,1,32,4096]{3,2,1,0:T(8,128)}, f32[1320,128]{1,0:T(8,128)S(1)}, f32[1320,128]{1,0:T(8,128)S(1)}, f32[1320,128]{1,0:T(8,128)S(1)}, f32[1320,128]{1,0:T(8,128)S(1)}) custom-call(bf16[1,1,24,4096]{3,2,1,0:T(8,128)(2,1)S(1)} %collective-permute-done.a_ref, ...), custom_call_target="tpu_custom_call", output_to_operand_aliasing={{1}: (3, {}), {2}: (4, {}), {3}: (5, {}), {4}: (6, {})} | custom-call | flops 600000000 | bytes 4000000 | tf_op jit(solution)/shard_map/moved/pallas_call | solution.py:161
  17.0 0.2 %all-to-all-done = f32[32,1,128]{2,1,0:T(1,128)S(1)} async-done(((f32[32,1,128]{2,1,0:T(1,128)}), f32[32,1,128]{2,1,0:T(1,128)S(1)}, u32[]{:S(2)}, u32[]{:S(2)}) %all-to-all-start) | async-done | bytes 16416 | tf_op jit(solution)/shard_map/all_to_all | solution.py:204
  17.2 0.6 %multiply_reduce_fusion = f32[]{:T(128)} fusion(f32[32,1,128]{2,1,0:T(1,128)S(1)} %all-to-all-done), kind=kLoop, calls=%fused_computation | loop fusion | flops 8191 | bytes 16388 | tf_op jit(solution)/shard_map/reduce_sum | solution.py:208
  (4 shorter events, 0.0 us)
Async XLA Ops:
  2.3 5.1 %copy-start = (bf16[1,1,24,4096]{3,2,1,0:T(8,128)(2,1)S(1)}, bf16[1,1,24,4096]{3,2,1,0:T(8,128)(2,1)}, u32[]{:S(2)}) copy-start(bf16[1,1,24,4096]{3,2,1,0:T(8,128)(2,1)} %a_ref.5) | copy-start | bytes 589828
  2.3 10.8 %collective-permute-start = (bf16[1,1,24,4096]{3,2,1,0:T(8,128)(2,1)}, bf16[1,1,24,4096]{3,2,1,0:T(8,128)(2,1)S(1)}, u32[]{:S(2)}, u32[]{:S(2)}) collective-permute-start(bf16[1,1,24,4096]{3,2,1,0:T(8,128)(2,1)} %a_ref.5), channel_id=1, source_target_pairs={{1,0},{2,1},{3,2},{4,3},{5,4},{6,5},{7,6},{0,7},{9,8},{10,9},{11,1... | collective-permute-start | bytes 589832 | tf_op jit(solution)/shard_map/ppermute | solution.py:30
  6.8 3.3 %copy-start.2 = (bf16[1,1,24,4096]{3,2,1,0:T(8,128)(2,1)S(1)}, bf16[1,1,24,4096]{3,2,1,0:T(8,128)(2,1)}, u32[]{:S(2)}) copy-start(bf16[1,1,24,4096]{3,2,1,0:T(8,128)(2,1)} %b_ref.1) | copy-start | bytes 589828
  6.8 6.3 %collective-permute-start.1 = (bf16[1,1,24,4096]{3,2,1,0:T(8,128)(2,1)}, bf16[1,1,24,4096]{3,2,1,0:T(8,128)(2,1)S(1)}, u32[]{:S(2)}, u32[]{:S(2)}) collective-permute-start(bf16[1,1,24,4096]{3,2,1,0:T(8,128)(2,1)} %b_ref.1), channel_id=1, source_target_pairs={{8,0},{16,8},{24,16},{0,24},{9,1},{17,9},{25,17},{1,25},{10,2},{18... | collective-permute-start | bytes 589832 | tf_op jit(solution)/shard_map/ppermute | solution.py:30
  7.4 2.6 %copy-start.1 = (s32[1,1,2,3,384]{4,2,3,1,0:T(2,128)S(1)}, s32[1,1,2,3,384]{4,2,3,1,0:T(2,128)}, u32[]{:S(2)}) copy-start(s32[1,1,2,3,384]{4,2,3,1,0:T(2,128)} %param.5) | copy-start | bytes 27652
  7.5 9.7 %all-to-all-start = ((f32[32,1,128]{2,1,0:T(1,128)}), f32[32,1,128]{2,1,0:T(1,128)S(1)}, u32[]{:S(2)}, u32[]{:S(2)}) async-start(f32[32,1,128]{2,1,0:T(1,128)} %squares_late.1), calls=%async_computation | async-start | bytes 32768 | tf_op jit(solution)/shard_map/all_to_all | solution.py:204

commit v6 on v5

--- a/solution.py
+++ b/solution.py
@@ -69,10 +69,12 @@
     listed[...] = (right_slot * NNZ + left_slot) * (PAIRS << SHIFT) + product_slot * APART
     copy = pltpu.make_async_copy(listed.at[0], place, sem)
     copy.start()
-    return copy
-
-
-def add_products(a_ref, b_ref, places, arriving, wide, left, pairs, totals):
+    behind = lax.broadcasted_iota(jnp.int32, listed.shape, 1) + 1
+    used = jnp.max(jnp.where(product_slot < NC, behind, 0))
+    return copy, (used + UNROLL - 1) // UNROLL
+
+
+def add_products(a_ref, b_ref, places, arriving, turns, wide, left, pairs, totals):
     for t in range(PAIRS):
         wide[pl.ds(t, NNZ, stride=APART), :] = a_ref[0, 0, :, t * LANES : (t + 1) * LANES].astype(jnp.float32)
     for n in range(NNZ):
@@ -109,23 +111,23 @@
             total[pl.ds(to, PAIRS), :] = total[pl.ds(to, PAIRS), :] + pairs[pl.ds(at, PAIRS), :]
         return carry
 
-    lax.fori_loop(0, places.shape[0] // UNROLL, add_entries, 0)
+    lax.fori_loop(0, turns, add_entries, 0)
 
 
 def own_kernel(a_ref, b_ref, slots_ref, *rest):
     totals = rest[:TOTALS]
     listed, place, wide, left, pairs, sem = rest[TOTALS:]
-    copy = send_list(slots_ref, 0, listed, place, sem)
+    copy, turns = send_list(slots_ref, 0, listed, place, sem)
     for total in totals:
         total[...] = jnp.zeros_like(total)
-    add_products(a_ref, b_ref, place, copy, wide, left, pairs, totals)
+    add_products(a_ref, b_ref, place, copy, turns, wide, left, pairs, totals)
 
 
 def moved_kernel(a_ref, b_ref, slots_ref, *rest):
     _, out_ref, totals = rest[:TOTALS], rest[TOTALS], rest[TOTALS + 1 : 2 * TOTALS + 1]
     listed, place, wide, left, pairs, sem = rest[2 * TOTALS + 1 :]
-    copy = send_list(slots_ref, 1, listed, place, sem)
-    add_products(a_ref, b_ref, place, copy, wide, left, pairs, totals)
+    copy, turns = send_list(slots_ref, 1, listed, place, sem)
+    add_products(a_ref, b_ref, place, copy, turns, wide, left, pairs, totals)
 
     for c in range(NC):
         rows = slice(c * APART, c * APART + PAIRS)

time: 18 us -> 18 us (level)
  Pallas kernels: 8.48 us -> 7.96 us
  waiting for transfers between devices: 0.21 us -> 0.73 us
    all_to_all x1, waiting for transfers between devices: 0.2 us -> 0.72 us  [per_device(): everyone = lax.all_to_all(ready, ('row', 'col'), 0, 0, tiled=True)]
    pallas_call x1, Pallas kernels: 3.83 us -> 3.41 us  [both_products(): pl.pallas_call(moved_kernel, out_shape=(jax.ShapeDtypeStruct((1, 1, NC, B...]
  transfers between devices with their start and end apart: 3 -> 3, of which waited for: 1 -> 1; matrix products, arithmetic and copies ran while one was open for 0% -> 0% of each run, Pallas kernels for 39% -> 36%
where the time goes in v6:
time: 18 us; the launch traced here: 17.8 us
  Pallas kernels  7.96 us (44%)
  starting transfers between devices  7.71 us (43%)
  waiting for transfers between devices  0.73 us (4%)
  between operations  0.73 us (4%)
  other arithmetic  0.63 us (4%)
    ppermute x2, starting transfers between devices, passed_along(): return lax.ppermute(block, axis, route)  5.13 us
    pallas_call x1, Pallas kernels, both_products(): pl.pallas_call(moved_kernel, out_shape=(jax.ShapeDtypeStruct((1, 1, NC, B...  3.41 us
    pallas_call x1, Pallas kernels, both_products(): pl.pallas_call(own_kernel, out_shape=(total,) * TOTALS, in_specs=[VMEM] *...  2.92 us
    all_to_all x1, starting transfers between devices, per_device(): everyone = lax.all_to_all(ready, ('row', 'col'), 0, 0, tiled=True)  2.58 us
    pallas_call x2, Pallas kernels, squares(): pl.pallas_call(functools.partial(squares_kernel, first_column), out_shape...  1.63 us
    all_to_all x1, waiting for transfers between devices, per_device(): everyone = lax.all_to_all(ready, ('row', 'col'), 0, 0, tiled=True)  0.72 us
    reduce_sum x1, other arithmetic, per_device(): norm_sq = jnp.sum(everyone * jnp.float32(1.0 / (count * NNZ * BS)))  0.63 us
  transfers between devices with their start and end apart: 3, of which 1 were waited for; matrix products, arithmetic and copies ran while one was open for 0% of the time, Pallas kernels for 36%

profile of v6, /device:TPU:0, one launch (start us, length us, event | category | flops | bytes accessed | tf_op | source)
XLA Modules:
  0.0 17.8 jit_solution(9390448232876153991)
XLA Ops:
  0.6 1.6 %squares_early.1.token_ref.rest_0_ = f32[32,1,128]{2,1,0:T(1,128)} custom-call(bf16[1,1,24,4096]{3,2,1,0:T(8,128)(2,1)} %a_ref.5), custom_call_target="tpu_custom_call" | custom-call | tf_op jit(solution)/shard_map/squares_early/pallas_call | solution.py:176
  2.3 0.0 copy-start
  2.3 4.5 %collective-permute-start = (bf16[1,1,24,4096]{3,2,1,0:T(8,128)(2,1)}, bf16[1,1,24,4096]{3,2,1,0:T(8,128)(2,1)S(1)}, u32[]{:S(2)}, u32[]{:S(2)}) collective-permute-start(bf16[1,1,24,4096]{3,2,1,0:T(8,128)(2,1)} %a_ref.5), channel_id=1, source_target_pairs={{1,0},{2,1},{3,2},{4,3},{5,4},{6,5},{7,6},{0,7},{9,8},{10,9},{11,1... | collective-permute-start | bytes 589832 | tf_op jit(solution)/shard_map/ppermute | solution.py:30
  6.8 0.0 copy-start.2
  6.8 0.7 %collective-permute-start.1 = (bf16[1,1,24,4096]{3,2,1,0:T(8,128)(2,1)}, bf16[1,1,24,4096]{3,2,1,0:T(8,128)(2,1)S(1)}, u32[]{:S(2)}, u32[]{:S(2)}) collective-permute-start(bf16[1,1,24,4096]{3,2,1,0:T(8,128)(2,1)} %b_ref.1), channel_id=1, source_target_pairs={{8,0},{16,8},{24,16},{0,24},{9,1},{17,9},{25,17},{1,25},{10,2},{18... | collective-permute-start | bytes 589832 | tf_op jit(solution)/shard_map/ppermute | solution.py:30
  7.4 0.0 copy-done
  7.4 0.0 copy-start.1
  7.5 2.6 %all-to-all-start = ((f32[32,1,128]{2,1,0:T(1,128)}), f32[32,1,128]{2,1,0:T(1,128)S(1)}, u32[]{:S(2)}, u32[]{:S(2)}) async-start(f32[32,1,128]{2,1,0:T(1,128)} %squares_late.1), calls=%async_computation | async-start | bytes 32768 | tf_op jit(solution)/shard_map/all_to_all | solution.py:206
  10.0 0.0 copy-done.2
  10.1 0.0 copy-done.1
  10.1 2.9 %own.1 = (f32[1320,128]{1,0:T(8,128)S(1)}, f32[1320,128]{1,0:T(8,128)S(1)}, f32[1320,128]{1,0:T(8,128)S(1)}, f32[1320,128]{1,0:T(8,128)S(1)}) custom-call(bf16[1,1,24,4096]{3,2,1,0:T(8,128)(2,1)S(1)} %copy-done, bf16[1,1,24,4096]{3,2,1,0:T(8,128)(2,1)S(1)} %copy-done.2, s32[1,1,3,2,384]{4,3,2,1,0:T(2,128)S(1)} %bitcast.1), custom_call_target="tpu_custom_call" | custom-call | flops 600000000 | bytes 4000000 | tf_op jit(solution)/shard_map/own/pallas_call | solution.py:155
  13.0 0.0 collective-permute-done.a_ref
  13.0 0.0 collective-permute-done.1.b_ref
  13.0 3.4 %moved.1 = (f32[1,1,32,4096]{3,2,1,0:T(8,128)}, f32[1320,128]{1,0:T(8,128)S(1)}, f32[1320,128]{1,0:T(8,128)S(1)}, f32[1320,128]{1,0:T(8,128)S(1)}, f32[1320,128]{1,0:T(8,128)S(1)}) custom-call(bf16[1,1,24,4096]{3,2,1,0:T(8,128)(2,1)S(1)} %collective-permute-done.a_ref, ...), custom_call_target="tpu_custom_call", output_to_operand_aliasing={{1}: (3, {}), {2}: (4, {}), {3}: (5, {}), {4}: (6, {})} | custom-call | flops 600000000 | bytes 4000000 | tf_op jit(solution)/shard_map/moved/pallas_call | solution.py:163
  16.4 0.7 %all-to-all-done = f32[32,1,128]{2,1,0:T(1,128)S(1)} async-done(((f32[32,1,128]{2,1,0:T(1,128)}), f32[32,1,128]{2,1,0:T(1,128)S(1)}, u32[]{:S(2)}, u32[]{:S(2)}) %all-to-all-start) | async-done | bytes 16416 | tf_op jit(solution)/shard_map/all_to_all | solution.py:206
  17.2 0.6 %multiply_reduce_fusion = f32[]{:T(128)} fusion(f32[32,1,128]{2,1,0:T(1,128)S(1)} %all-to-all-done), kind=kLoop, calls=%fused_computation | loop fusion | flops 8191 | bytes 16388 | tf_op jit(solution)/shard_map/reduce_sum | solution.py:210
  (4 shorter events, 0.0 us)
Async XLA Ops:
  2.3 5.1 %copy-start = (bf16[1,1,24,4096]{3,2,1,0:T(8,128)(2,1)S(1)}, bf16[1,1,24,4096]{3,2,1,0:T(8,128)(2,1)}, u32[]{:S(2)}) copy-start(bf16[1,1,24,4096]{3,2,1,0:T(8,128)(2,1)} %a_ref.5) | copy-start | bytes 589828
  2.3 10.7 %collective-permute-start = (bf16[1,1,24,4096]{3,2,1,0:T(8,128)(2,1)}, bf16[1,1,24,4096]{3,2,1,0:T(8,128)(2,1)S(1)}, u32[]{:S(2)}, u32[]{:S(2)}) collective-permute-start(bf16[1,1,24,4096]{3,2,1,0:T(8,128)(2,1)} %a_ref.5), channel_id=1, source_target_pairs={{1,0},{2,1},{3,2},{4,3},{5,4},{6,5},{7,6},{0,7},{9,8},{10,9},{11,1... | collective-permute-start | bytes 589832 | tf_op jit(solution)/shard_map/ppermute | solution.py:30
  6.8 3.3 %copy-start.2 = (bf16[1,1,24,4096]{3,2,1,0:T(8,128)(2,1)S(1)}, bf16[1,1,24,4096]{3,2,1,0:T(8,128)(2,1)}, u32[]{:S(2)}) copy-start(bf16[1,1,24,4096]{3,2,1,0:T(8,128)(2,1)} %b_ref.1) | copy-start | bytes 589828
  6.8 6.2 %collective-permute-start.1 = (bf16[1,1,24,4096]{3,2,1,0:T(8,128)(2,1)}, bf16[1,1,24,4096]{3,2,1,0:T(8,128)(2,1)S(1)}, u32[]{:S(2)}, u32[]{:S(2)}) collective-permute-start(bf16[1,1,24,4096]{3,2,1,0:T(8,128)(2,1)} %b_ref.1), channel_id=1, source_target_pairs={{8,0},{16,8},{24,16},{0,24},{9,1},{17,9},{25,17},{1,25},{10,2},{18... | collective-permute-start | bytes 589832 | tf_op jit(solution)/shard_map/ppermute | solution.py:30
  7.4 2.6 %copy-start.1 = (s32[1,1,2,3,384]{4,2,3,1,0:T(2,128)S(1)}, s32[1,1,2,3,384]{4,2,3,1,0:T(2,128)}, u32[]{:S(2)}) copy-start(s32[1,1,2,3,384]{4,2,3,1,0:T(2,128)} %param.5) | copy-start | bytes 27652
  7.5 9.7 %all-to-all-start = ((f32[32,1,128]{2,1,0:T(1,128)}), f32[32,1,128]{2,1,0:T(1,128)S(1)}, u32[]{:S(2)}, u32[]{:S(2)}) async-start(f32[32,1,128]{2,1,0:T(1,128)} %squares_late.1), calls=%async_computation | async-start | bytes 32768 | tf_op jit(solution)/shard_map/all_to_all | solution.py:206

commit v7 on v6

--- a/solution.py
+++ b/solution.py
@@ -199,7 +199,7 @@
     first = after(after(ready, "first", FULL_VMEM), "second", FULL_VMEM)
     first, a_after = lax.optimization_barrier((first, a_blocks))
     a_moved = passed_along(a_after, "col", -1)
-    third = after(ready, "third", SOME_VMEM, 8192)
+    third = after(ready, "third", SOME_VMEM, 49152)
     third, b_after = lax.optimization_barrier((third, b_blocks))
     b_moved = passed_along(b_after, "row", -1)
     ready = squares(a_blocks, count, (ready, first, third))

time: 18 us -> 17.8 us (0.989)
    pallas_call x1, Pallas kernels: 3.41 us -> 3.8 us  [both_products(): pl.pallas_call(moved_kernel, out_shape=(jax.ShapeDtypeStruct((1, 1, NC, B...]
    pallas_call x1, Pallas kernels: 2.92 us -> 2.54 us  [both_products(): pl.pallas_call(own_kernel, out_shape=(total,) * TOTALS, in_specs=[VMEM] *...]
where the time goes in v7:
time: 17.8 us; the launch traced here: 17.6 us
  Pallas kernels  7.97 us (45%)
  starting transfers between devices  7.7 us (43%)
  between operations  0.73 us (4%)
  other arithmetic  0.63 us (4%)
  waiting for transfers between devices  0.59 us (3%)
    ppermute x2, starting transfers between devices, passed_along(): return lax.ppermute(block, axis, route)  5.13 us
    pallas_call x1, Pallas kernels, both_products(): pl.pallas_call(moved_kernel, out_shape=(jax.ShapeDtypeStruct((1, 1, NC, B...  3.8 us
    all_to_all x1, starting transfers between devices, per_device(): everyone = lax.all_to_all(ready, ('row', 'col'), 0, 0, tiled=True)  2.57 us
    pallas_call x1, Pallas kernels, both_products(): pl.pallas_call(own_kernel, out_shape=(total,) * TOTALS, in_specs=[VMEM] *...  2.54 us
    pallas_call x2, Pallas kernels, squares(): pl.pallas_call(functools.partial(squares_kernel, first_column), out_shape...  1.62 us
    reduce_sum x1, other arithmetic, per_device(): norm_sq = jnp.sum(everyone * jnp.float32(1.0 / (count * NNZ * BS)))  0.63 us
    all_to_all x1, waiting for transfers between devices, per_device(): everyone = lax.all_to_all(ready, ('row', 'col'), 0, 0, tiled=True)  0.58 us
  transfers between devices with their start and end apart: 3, of which 1 were waited for; matrix products, arithmetic and copies ran while one was open for 0% of the time, Pallas kernels for 36%

profile of v7, /device:TPU:0, one launch (start us, length us, event | category | flops | bytes accessed | tf_op | source)
XLA Modules:
  0.0 17.6 jit_solution(17446698225471358971)
XLA Ops:
  0.6 1.6 %squares_early.1.token_ref.rest_0_ = f32[32,1,128]{2,1,0:T(1,128)} custom-call(bf16[1,1,24,4096]{3,2,1,0:T(8,128)(2,1)} %a_ref.5), custom_call_target="tpu_custom_call" | custom-call | tf_op jit(solution)/shard_map/squares_early/pallas_call | solution.py:176
  2.3 0.0 copy-start.2
  2.3 0.0 copy-start
  2.3 0.0 copy-start.1
  2.3 4.5 %collective-permute-start = (bf16[1,1,24,4096]{3,2,1,0:T(8,128)(2,1)}, bf16[1,1,24,4096]{3,2,1,0:T(8,128)(2,1)S(1)}, u32[]{:S(2)}, u32[]{:S(2)}) collective-permute-start(bf16[1,1,24,4096]{3,2,1,0:T(8,128)(2,1)} %a_ref.5), channel_id=1, source_target_pairs={{1,0},{2,1},{3,2},{4,3},{5,4},{6,5},{7,6},{0,7},{9,8},{10,9},{11,1... | collective-permute-start | bytes 589832 | tf_op jit(solution)/shard_map/ppermute | solution.py:30
  6.8 0.0 copy-done.2
  6.8 0.7 %collective-permute-start.1 = (bf16[1,1,24,4096]{3,2,1,0:T(8,128)(2,1)S(1)}, bf16[1,1,24,4096]{3,2,1,0:T(8,128)(2,1)S(1)}, u32[]{:S(2)}, u32[]{:S(2)}) collective-permute-start(bf16[1,1,24,4096]{3,2,1,0:T(8,128)(2,1)S(1)} %copy-done.2), channel_id=1, source_target_pairs={{8,0},{16,8},{24,16},{0,24},{9,1},{17,9},{25,17},{1,25},{10,2},{18... | collective-permute-start | bytes 589832 | tf_op jit(solution)/shard_map/ppermute | solution.py:30
  7.4 0.0 copy-done
  7.5 2.6 %all-to-all-start = ((f32[32,1,128]{2,1,0:T(1,128)}), f32[32,1,128]{2,1,0:T(1,128)S(1)}, u32[]{:S(2)}, u32[]{:S(2)}) async-start(f32[32,1,128]{2,1,0:T(1,128)} %squares_late.1), calls=%async_computation | async-start | bytes 32768 | tf_op jit(solution)/shard_map/all_to_all | solution.py:206
  10.0 0.0 copy-done.1
  10.1 2.5 %own.1 = (f32[1320,128]{1,0:T(8,128)S(1)}, f32[1320,128]{1,0:T(8,128)S(1)}, f32[1320,128]{1,0:T(8,128)S(1)}, f32[1320,128]{1,0:T(8,128)S(1)}) custom-call(bf16[1,1,24,4096]{3,2,1,0:T(8,128)(2,1)S(1)} %copy-done, bf16[1,1,24,4096]{3,2,1,0:T(8,128)(2,1)S(1)} %copy-done.2, s32[1,1,3,2,384]{4,3,2,1,0:T(2,128)S(1)} %bitcast.1), custom_call_target="tpu_custom_call" | custom-call | flops 600000000 | bytes 4000000 | tf_op jit(solution)/shard_map/own/pallas_call | solution.py:155
  12.6 0.0 collective-permute-done.a_ref
  12.6 0.0 collective-permute-done.1.b_ref
  12.6 3.8 %moved.1 = (f32[1,1,32,4096]{3,2,1,0:T(8,128)}, f32[1320,128]{1,0:T(8,128)S(1)}, f32[1320,128]{1,0:T(8,128)S(1)}, f32[1320,128]{1,0:T(8,128)S(1)}, f32[1320,128]{1,0:T(8,128)S(1)}) custom-call(bf16[1,1,24,4096]{3,2,1,0:T(8,128)(2,1)S(1)} %collective-permute-done.a_ref, ...), custom_call_target="tpu_custom_call", output_to_operand_aliasing={{1}: (3, {}), {2}: (4, {}), {3}: (5, {}), {4}: (6, {})} | custom-call | flops 600000000 | bytes 4000000 | tf_op jit(solution)/shard_map/moved/pallas_call | solution.py:163
  16.4 0.6 %all-to-all-done = f32[32,1,128]{2,1,0:T(1,128)S(1)} async-done(((f32[32,1,128]{2,1,0:T(1,128)}), f32[32,1,128]{2,1,0:T(1,128)S(1)}, u32[]{:S(2)}, u32[]{:S(2)}) %all-to-all-start) | async-done | bytes 16416 | tf_op jit(solution)/shard_map/all_to_all | solution.py:206
  17.0 0.6 %multiply_reduce_fusion = f32[]{:T(128)} fusion(f32[32,1,128]{2,1,0:T(1,128)S(1)} %all-to-all-done), kind=kLoop, calls=%fused_computation | loop fusion | flops 8191 | bytes 16388 | tf_op jit(solution)/shard_map/reduce_sum | solution.py:210
  (4 shorter events, 0.0 us)
Async XLA Ops:
  2.3 4.5 %copy-start.2 = (bf16[1,1,24,4096]{3,2,1,0:T(8,128)(2,1)S(1)}, bf16[1,1,24,4096]{3,2,1,0:T(8,128)(2,1)}, u32[]{:S(2)}) copy-start(bf16[1,1,24,4096]{3,2,1,0:T(8,128)(2,1)} %b_ref.1) | copy-start | bytes 589828
  2.3 5.2 %copy-start = (bf16[1,1,24,4096]{3,2,1,0:T(8,128)(2,1)S(1)}, bf16[1,1,24,4096]{3,2,1,0:T(8,128)(2,1)}, u32[]{:S(2)}) copy-start(bf16[1,1,24,4096]{3,2,1,0:T(8,128)(2,1)} %a_ref.5) | copy-start | bytes 589828
  2.3 7.8 %copy-start.1 = (s32[1,1,2,3,384]{4,2,3,1,0:T(2,128)S(1)}, s32[1,1,2,3,384]{4,2,3,1,0:T(2,128)}, u32[]{:S(2)}) copy-start(s32[1,1,2,3,384]{4,2,3,1,0:T(2,128)} %param.5) | copy-start | bytes 27652
  2.3 10.3 %collective-permute-start = (bf16[1,1,24,4096]{3,2,1,0:T(8,128)(2,1)}, bf16[1,1,24,4096]{3,2,1,0:T(8,128)(2,1)S(1)}, u32[]{:S(2)}, u32[]{:S(2)}) collective-permute-start(bf16[1,1,24,4096]{3,2,1,0:T(8,128)(2,1)} %a_ref.5), channel_id=1, source_target_pairs={{1,0},{2,1},{3,2},{4,3},{5,4},{6,5},{7,6},{0,7},{9,8},{10,9},{11,1... | collective-permute-start | bytes 589832 | tf_op jit(solution)/shard_map/ppermute | solution.py:30
  6.8 5.8 %collective-permute-start.1 = (bf16[1,1,24,4096]{3,2,1,0:T(8,128)(2,1)S(1)}, bf16[1,1,24,4096]{3,2,1,0:T(8,128)(2,1)S(1)}, u32[]{:S(2)}, u32[]{:S(2)}) collective-permute-start(bf16[1,1,24,4096]{3,2,1,0:T(8,128)(2,1)S(1)} %copy-done.2), channel_id=1, source_target_pairs={{8,0},{16,8},{24,16},{0,24},{9,1},{17,9},{25,17},{1,25},{10,2},{18... | collective-permute-start | bytes 589832 | tf_op jit(solution)/shard_map/ppermute | solution.py:30
  7.5 9.5 %all-to-all-start = ((f32[32,1,128]{2,1,0:T(1,128)}), f32[32,1,128]{2,1,0:T(1,128)S(1)}, u32[]{:S(2)}, u32[]{:S(2)}) async-start(f32[32,1,128]{2,1,0:T(1,128)} %squares_late.1), calls=%async_computation | async-start | bytes 32768 | tf_op jit(solution)/shard_map/all_to_all | solution.py:206

commit v8 on v7

--- a/solution.py
+++ b/solution.py
@@ -196,13 +196,11 @@
 def per_device(a_blocks, b_blocks, products):
     count = lax.axis_size("row") * lax.axis_size("col")
     ready = squares(a_blocks, count)
-    first = after(after(ready, "first", FULL_VMEM), "second", FULL_VMEM)
-    first, a_after = lax.optimization_barrier((first, a_blocks))
+    ready, a_after = lax.optimization_barrier((ready, a_blocks))
     a_moved = passed_along(a_after, "col", -1)
     third = after(ready, "third", SOME_VMEM, 49152)
-    third, b_after = lax.optimization_barrier((third, b_blocks))
-    b_moved = passed_along(b_after, "row", -1)
-    ready = squares(a_blocks, count, (ready, first, third))
+    b_moved = passed_along(b_blocks, "row", -1)
+    ready = squares(a_blocks, count, (ready, third))
     everyone = lax.all_to_all(ready, ("row", "col"), 0, 0, tiled=True)
     a_near, b_near = (pltpu.with_memory_space_constraint(x, pltpu.VMEM) for x in (a_blocks, b_blocks))
     product = both_products(a_near, b_near, a_moved, b_moved, products)

time: 17.8 us -> 17.8 us (level)
  no operation moved by 1% of the time
where the time goes in v8:
time: 17.8 us; the launch traced here: 17.6 us
  Pallas kernels  7.92 us (44%)
  starting transfers between devices  7.7 us (43%)
  between operations  0.73 us (4%)
  other arithmetic  0.63 us (4%)
  waiting for transfers between devices  0.61 us (3%)
    ppermute x2, starting transfers between devices, passed_along(): return lax.ppermute(block, axis, route)  5.13 us
    pallas_call x1, Pallas kernels, both_products(): pl.pallas_call(moved_kernel, out_shape=(jax.ShapeDtypeStruct((1, 1, NC, B...  3.7 us
    pallas_call x1, Pallas kernels, both_products(): pl.pallas_call(own_kernel, out_shape=(total,) * TOTALS, in_specs=[VMEM] *...  2.59 us
    all_to_all x1, starting transfers between devices, per_device(): everyone = lax.all_to_all(ready, ('row', 'col'), 0, 0, tiled=True)  2.57 us
    pallas_call x2, Pallas kernels, squares(): pl.pallas_call(functools.partial(squares_kernel, first_column), out_shape...  1.62 us
    reduce_sum x1, other arithmetic, per_device(): norm_sq = jnp.sum(everyone * jnp.float32(1.0 / (count * NNZ * BS)))  0.63 us
    all_to_all x1, waiting for transfers between devices, per_device(): everyone = lax.all_to_all(ready, ('row', 'col'), 0, 0, tiled=True)  0.61 us
  transfers between devices with their start and end apart: 3, of which 1 were waited for; matrix products, arithmetic and copies ran while one was open for 0% of the time, Pallas kernels for 36%

profile of v8, /device:TPU:0, one launch (start us, length us, event | category | flops | bytes accessed | tf_op | source)
XLA Modules:
  0.0 17.6 jit_solution(1745203774926306214)
XLA Ops:
  0.6 1.6 %squares_early.1.token_ref.rest_0_ = f32[32,1,128]{2,1,0:T(1,128)} custom-call(bf16[1,1,24,4096]{3,2,1,0:T(8,128)(2,1)} %a_ref.5), custom_call_target="tpu_custom_call" | custom-call | tf_op jit(solution)/shard_map/squares_early/pallas_call | solution.py:176
  2.2 0.0 copy-start
  2.3 0.0 copy-start.1
  2.3 0.0 copy-start.2
  2.3 4.5 %collective-permute-start = (bf16[1,1,24,4096]{3,2,1,0:T(8,128)(2,1)}, bf16[1,1,24,4096]{3,2,1,0:T(8,128)(2,1)S(1)}, u32[]{:S(2)}, u32[]{:S(2)}) collective-permute-start(bf16[1,1,24,4096]{3,2,1,0:T(8,128)(2,1)} %a_ref.5), channel_id=1, source_target_pairs={{1,0},{2,1},{3,2},{4,3},{5,4},{6,5},{7,6},{0,7},{9,8},{10,9},{11,1... | collective-permute-start | bytes 589832 | tf_op jit(solution)/shard_map/ppermute | solution.py:30
  6.8 0.7 %collective-permute-start.1 = (bf16[1,1,24,4096]{3,2,1,0:T(8,128)(2,1)}, bf16[1,1,24,4096]{3,2,1,0:T(8,128)(2,1)S(1)}, u32[]{:S(2)}, u32[]{:S(2)}) collective-permute-start(bf16[1,1,24,4096]{3,2,1,0:T(8,128)(2,1)} %b_ref.1), channel_id=1, source_target_pairs={{8,0},{16,8},{24,16},{0,24},{9,1},{17,9},{25,17},{1,25},{10,2},{18... | collective-permute-start | bytes 589832 | tf_op jit(solution)/shard_map/ppermute | solution.py:30
  7.4 0.0 copy-done
  7.4 2.6 %all-to-all-start = ((f32[32,1,128]{2,1,0:T(1,128)}), f32[32,1,128]{2,1,0:T(1,128)S(1)}, u32[]{:S(2)}, u32[]{:S(2)}) async-start(f32[32,1,128]{2,1,0:T(1,128)} %squares_late.1), calls=%async_computation | async-start | bytes 32768 | tf_op jit(solution)/shard_map/all_to_all | solution.py:204
  10.0 0.0 copy-done.1
  10.0 0.0 copy-done.2
  10.0 2.6 %own.1 = (f32[1320,128]{1,0:T(8,128)S(1)}, f32[1320,128]{1,0:T(8,128)S(1)}, f32[1320,128]{1,0:T(8,128)S(1)}, f32[1320,128]{1,0:T(8,128)S(1)}) custom-call(bf16[1,1,24,4096]{3,2,1,0:T(8,128)(2,1)S(1)} %copy-done, bf16[1,1,24,4096]{3,2,1,0:T(8,128)(2,1)S(1)} %copy-done.2, s32[1,1,3,2,384]{4,3,2,1,0:T(2,128)S(1)} %bitcast.1), custom_call_target="tpu_custom_call" | custom-call | flops 600000000 | bytes 4000000 | tf_op jit(solution)/shard_map/own/pallas_call | solution.py:155
  12.6 0.0 collective-permute-done.a_ref
  12.7 0.0 collective-permute-done.1.b_ref
  12.7 3.7 %moved.1 = (f32[1,1,32,4096]{3,2,1,0:T(8,128)}, f32[1320,128]{1,0:T(8,128)S(1)}, f32[1320,128]{1,0:T(8,128)S(1)}, f32[1320,128]{1,0:T(8,128)S(1)}, f32[1320,128]{1,0:T(8,128)S(1)}) custom-call(bf16[1,1,24,4096]{3,2,1,0:T(8,128)(2,1)S(1)} %collective-permute-done.a_ref, ...), custom_call_target="tpu_custom_call", output_to_operand_aliasing={{1}: (3, {}), {2}: (4, {}), {3}: (5, {}), {4}: (6, {})} | custom-call | flops 600000000 | bytes 4000000 | tf_op jit(solution)/shard_map/moved/pallas_call | solution.py:163
  16.4 0.6 %all-to-all-done = f32[32,1,128]{2,1,0:T(1,128)S(1)} async-done(((f32[32,1,128]{2,1,0:T(1,128)}), f32[32,1,128]{2,1,0:T(1,128)S(1)}, u32[]{:S(2)}, u32[]{:S(2)}) %all-to-all-start) | async-done | bytes 16416 | tf_op jit(solution)/shard_map/all_to_all | solution.py:204
  17.0 0.6 %multiply_reduce_fusion = f32[]{:T(128)} fusion(f32[32,1,128]{2,1,0:T(1,128)S(1)} %all-to-all-done), kind=kLoop, calls=%fused_computation | loop fusion | flops 8191 | bytes 16388 | tf_op jit(solution)/shard_map/reduce_sum | solution.py:208
  (2 shorter events, 0.0 us)
Async XLA Ops:
  2.2 5.2 %copy-start = (bf16[1,1,24,4096]{3,2,1,0:T(8,128)(2,1)S(1)}, bf16[1,1,24,4096]{3,2,1,0:T(8,128)(2,1)}, u32[]{:S(2)}) copy-start(bf16[1,1,24,4096]{3,2,1,0:T(8,128)(2,1)} %a_ref.5) | copy-start | bytes 589828
  2.3 7.8 %copy-start.1 = (s32[1,1,2,3,384]{4,2,3,1,0:T(2,128)S(1)}, s32[1,1,2,3,384]{4,2,3,1,0:T(2,128)}, u32[]{:S(2)}) copy-start(s32[1,1,2,3,384]{4,2,3,1,0:T(2,128)} %param.5) | copy-start | bytes 27652
  2.3 7.8 %copy-start.2 = (bf16[1,1,24,4096]{3,2,1,0:T(8,128)(2,1)S(1)}, bf16[1,1,24,4096]{3,2,1,0:T(8,128)(2,1)}, u32[]{:S(2)}) copy-start(bf16[1,1,24,4096]{3,2,1,0:T(8,128)(2,1)} %b_ref.1) | copy-start | bytes 589828
  2.3 10.4 %collective-permute-start = (bf16[1,1,24,4096]{3,2,1,0:T(8,128)(2,1)}, bf16[1,1,24,4096]{3,2,1,0:T(8,128)(2,1)S(1)}, u32[]{:S(2)}, u32[]{:S(2)}) collective-permute-start(bf16[1,1,24,4096]{3,2,1,0:T(8,128)(2,1)} %a_ref.5), channel_id=1, source_target_pairs={{1,0},{2,1},{3,2},{4,3},{5,4},{6,5},{7,6},{0,7},{9,8},{10,9},{11,1... | collective-permute-start | bytes 589832 | tf_op jit(solution)/shard_map/ppermute | solution.py:30
  6.8 5.9 %collective-permute-start.1 = (bf16[1,1,24,4096]{3,2,1,0:T(8,128)(2,1)}, bf16[1,1,24,4096]{3,2,1,0:T(8,128)(2,1)S(1)}, u32[]{:S(2)}, u32[]{:S(2)}) collective-permute-start(bf16[1,1,24,4096]{3,2,1,0:T(8,128)(2,1)} %b_ref.1), channel_id=1, source_target_pairs={{8,0},{16,8},{24,16},{0,24},{9,1},{17,9},{25,17},{1,25},{10,2},{18... | collective-permute-start | bytes 589832 | tf_op jit(solution)/shard_map/ppermute | solution.py:30
  7.4 9.5 %all-to-all-start = ((f32[32,1,128]{2,1,0:T(1,128)}), f32[32,1,128]{2,1,0:T(1,128)S(1)}, u32[]{:S(2)}, u32[]{:S(2)}) async-start(f32[32,1,128]{2,1,0:T(1,128)} %squares_late.1), calls=%async_computation | async-start | bytes 32768 | tf_op jit(solution)/shard_map/all_to_all | solution.py:204

commit v9 on v8

--- a/solution.py
+++ b/solution.py
@@ -119,7 +119,8 @@
     listed, place, wide, left, pairs, sem = rest[TOTALS:]
     copy, turns = send_list(slots_ref, 0, listed, place, sem)
     for total in totals:
-        total[...] = jnp.zeros_like(total)
+        for c in range(NC + 1):
+            total[c * APART : c * APART + PAIRS, :] = jnp.zeros((PAIRS, LANES), jnp.float32)
     add_products(a_ref, b_ref, place, copy, turns, wide, left, pairs, totals)
 
 

time: 17.8 us -> 17.8 us (level)
  waiting for transfers between devices: 0.61 us -> 0.9 us
  Pallas kernels: 7.92 us -> 7.64 us
    pallas_call x1, Pallas kernels: 3.7 us -> 3.42 us  [both_products(): pl.pallas_call(moved_kernel, out_shape=(jax.ShapeDtypeStruct((1, 1, NC, B...]
    all_to_all x1, waiting for transfers between devices: 0.61 us -> 0.89 us  [per_device(): everyone = lax.all_to_all(ready, ('row', 'col'), 0, 0, tiled=True)]
  transfers between devices with their start and end apart: 3 -> 3, of which waited for: 1 -> 1; matrix products, arithmetic and copies ran while one was open for 0% -> 0% of each run, Pallas kernels for 36% -> 34%
where the time goes in v9:
time: 17.8 us; the launch traced here: 17.6 us
  starting transfers between devices  7.7 us (43%)
  Pallas kernels  7.64 us (43%)
  waiting for transfers between devices  0.9 us (5%)
  between operations  0.73 us (4%)
  other arithmetic  0.63 us (4%)
    ppermute x2, starting transfers between devices, passed_along(): return lax.ppermute(block, axis, route)  5.13 us
    pallas_call x1, Pallas kernels, both_products(): pl.pallas_call(moved_kernel, out_shape=(jax.ShapeDtypeStruct((1, 1, NC, B...  3.42 us
    pallas_call x1, Pallas kernels, both_products(): pl.pallas_call(own_kernel, out_shape=(total,) * TOTALS, in_specs=[VMEM] *...  2.6 us
    all_to_all x1, starting transfers between devices, per_device(): everyone = lax.all_to_all(ready, ('row', 'col'), 0, 0, tiled=True)  2.57 us
    pallas_call x2, Pallas kernels, squares(): pl.pallas_call(functools.partial(squares_kernel, first_column), out_shape...  1.62 us
    all_to_all x1, waiting for transfers between devices, per_device(): everyone = lax.all_to_all(ready, ('row', 'col'), 0, 0, tiled=True)  0.89 us
    reduce_sum x1, other arithmetic, per_device(): norm_sq = jnp.sum(everyone * jnp.float32(1.0 / (count * NNZ * BS)))  0.63 us
  transfers between devices with their start and end apart: 3, of which 1 were waited for; matrix products, arithmetic and copies ran while one was open for 0% of the time, Pallas kernels for 34%

profile of v9, /device:TPU:0, one launch (start us, length us, event | category | flops | bytes accessed | tf_op | source)
XLA Modules:
  0.0 17.6 jit_solution(124378386852341799)
XLA Ops:
  0.6 1.6 %squares_early.1.token_ref.rest_0_ = f32[32,1,128]{2,1,0:T(1,128)} custom-call(bf16[1,1,24,4096]{3,2,1,0:T(8,128)(2,1)} %a_ref.5), custom_call_target="tpu_custom_call" | custom-call | tf_op jit(solution)/shard_map/squares_early/pallas_call | solution.py:177
  2.2 0.0 copy-start
  2.3 0.0 copy-start.1
  2.3 0.0 copy-start.2
  2.3 4.5 %collective-permute-start = (bf16[1,1,24,4096]{3,2,1,0:T(8,128)(2,1)}, bf16[1,1,24,4096]{3,2,1,0:T(8,128)(2,1)S(1)}, u32[]{:S(2)}, u32[]{:S(2)}) collective-permute-start(bf16[1,1,24,4096]{3,2,1,0:T(8,128)(2,1)} %a_ref.5), channel_id=1, source_target_pairs={{1,0},{2,1},{3,2},{4,3},{5,4},{6,5},{7,6},{0,7},{9,8},{10,9},{11,1... | collective-permute-start | bytes 589832 | tf_op jit(solution)/shard_map/ppermute | solution.py:30
  6.8 0.7 %collective-permute-start.1 = (bf16[1,1,24,4096]{3,2,1,0:T(8,128)(2,1)}, bf16[1,1,24,4096]{3,2,1,0:T(8,128)(2,1)S(1)}, u32[]{:S(2)}, u32[]{:S(2)}) collective-permute-start(bf16[1,1,24,4096]{3,2,1,0:T(8,128)(2,1)} %b_ref.1), channel_id=1, source_target_pairs={{8,0},{16,8},{24,16},{0,24},{9,1},{17,9},{25,17},{1,25},{10,2},{18... | collective-permute-start | bytes 589832 | tf_op jit(solution)/shard_map/ppermute | solution.py:30
  7.4 0.0 copy-done
  7.4 2.6 %all-to-all-start = ((f32[32,1,128]{2,1,0:T(1,128)}), f32[32,1,128]{2,1,0:T(1,128)S(1)}, u32[]{:S(2)}, u32[]{:S(2)}) async-start(f32[32,1,128]{2,1,0:T(1,128)} %squares_late.1), calls=%async_computation | async-start | bytes 32768 | tf_op jit(solution)/shard_map/all_to_all | solution.py:205
  10.0 0.0 copy-done.1
  10.0 0.0 copy-done.2
  10.0 2.6 %own.1 = (f32[1320,128]{1,0:T(8,128)S(1)}, f32[1320,128]{1,0:T(8,128)S(1)}, f32[1320,128]{1,0:T(8,128)S(1)}, f32[1320,128]{1,0:T(8,128)S(1)}) custom-call(bf16[1,1,24,4096]{3,2,1,0:T(8,128)(2,1)S(1)} %copy-done, bf16[1,1,24,4096]{3,2,1,0:T(8,128)(2,1)S(1)} %copy-done.2, s32[1,1,3,2,384]{4,3,2,1,0:T(2,128)S(1)} %bitcast.1), custom_call_target="tpu_custom_call" | custom-call | flops 600000000 | bytes 4000000 | tf_op jit(solution)/shard_map/own/pallas_call | solution.py:156
  12.6 0.0 collective-permute-done.a_ref
  12.7 0.0 collective-permute-done.1.b_ref
  12.7 3.4 %moved.1 = (f32[1,1,32,4096]{3,2,1,0:T(8,128)}, f32[1320,128]{1,0:T(8,128)S(1)}, f32[1320,128]{1,0:T(8,128)S(1)}, f32[1320,128]{1,0:T(8,128)S(1)}, f32[1320,128]{1,0:T(8,128)S(1)}) custom-call(bf16[1,1,24,4096]{3,2,1,0:T(8,128)(2,1)S(1)} %collective-permute-done.a_ref, ...), custom_call_target="tpu_custom_call", output_to_operand_aliasing={{1}: (3, {}), {2}: (4, {}), {3}: (5, {}), {4}: (6, {})} | custom-call | flops 600000000 | bytes 4000000 | tf_op jit(solution)/shard_map/moved/pallas_call | solution.py:164
  16.1 0.9 %all-to-all-done = f32[32,1,128]{2,1,0:T(1,128)S(1)} async-done(((f32[32,1,128]{2,1,0:T(1,128)}), f32[32,1,128]{2,1,0:T(1,128)S(1)}, u32[]{:S(2)}, u32[]{:S(2)}) %all-to-all-start) | async-done | bytes 16416 | tf_op jit(solution)/shard_map/all_to_all | solution.py:205
  17.0 0.6 %multiply_reduce_fusion = f32[]{:T(128)} fusion(f32[32,1,128]{2,1,0:T(1,128)S(1)} %all-to-all-done), kind=kLoop, calls=%fused_computation | loop fusion | flops 8191 | bytes 16388 | tf_op jit(solution)/shard_map/reduce_sum | solution.py:209
  (2 shorter events, 0.0 us)
Async XLA Ops:
  2.2 5.2 %copy-start = (bf16[1,1,24,4096]{3,2,1,0:T(8,128)(2,1)S(1)}, bf16[1,1,24,4096]{3,2,1,0:T(8,128)(2,1)}, u32[]{:S(2)}) copy-start(bf16[1,1,24,4096]{3,2,1,0:T(8,128)(2,1)} %a_ref.5) | copy-start | bytes 589828
  2.3 7.8 %copy-start.1 = (s32[1,1,2,3,384]{4,2,3,1,0:T(2,128)S(1)}, s32[1,1,2,3,384]{4,2,3,1,0:T(2,128)}, u32[]{:S(2)}) copy-start(s32[1,1,2,3,384]{4,2,3,1,0:T(2,128)} %param.5) | copy-start | bytes 27652
  2.3 7.8 %copy-start.2 = (bf16[1,1,24,4096]{3,2,1,0:T(8,128)(2,1)S(1)}, bf16[1,1,24,4096]{3,2,1,0:T(8,128)(2,1)}, u32[]{:S(2)}) copy-start(bf16[1,1,24,4096]{3,2,1,0:T(8,128)(2,1)} %b_ref.1) | copy-start | bytes 589828
  2.3 10.4 %collective-permute-start = (bf16[1,1,24,4096]{3,2,1,0:T(8,128)(2,1)}, bf16[1,1,24,4096]{3,2,1,0:T(8,128)(2,1)S(1)}, u32[]{:S(2)}, u32[]{:S(2)}) collective-permute-start(bf16[1,1,24,4096]{3,2,1,0:T(8,128)(2,1)} %a_ref.5), channel_id=1, source_target_pairs={{1,0},{2,1},{3,2},{4,3},{5,4},{6,5},{7,6},{0,7},{9,8},{10,9},{11,1... | collective-permute-start | bytes 589832 | tf_op jit(solution)/shard_map/ppermute | solution.py:30
  6.8 5.9 %collective-permute-start.1 = (bf16[1,1,24,4096]{3,2,1,0:T(8,128)(2,1)}, bf16[1,1,24,4096]{3,2,1,0:T(8,128)(2,1)S(1)}, u32[]{:S(2)}, u32[]{:S(2)}) collective-permute-start(bf16[1,1,24,4096]{3,2,1,0:T(8,128)(2,1)} %b_ref.1), channel_id=1, source_target_pairs={{8,0},{16,8},{24,16},{0,24},{9,1},{17,9},{25,17},{1,25},{10,2},{18... | collective-permute-start | bytes 589832 | tf_op jit(solution)/shard_map/ppermute | solution.py:30
  7.4 9.5 %all-to-all-start = ((f32[32,1,128]{2,1,0:T(1,128)}), f32[32,1,128]{2,1,0:T(1,128)S(1)}, u32[]{:S(2)}, u32[]{:S(2)}) async-start(f32[32,1,128]{2,1,0:T(1,128)} %squares_late.1), calls=%async_computation | async-start | bytes 32768 | tf_op jit(solution)/shard_map/all_to_all | solution.py:205
